TPU v7x, 128 devices: a whole 4x4x4 slice. The times are simulated.
128 devices in a mesh: dp: 4 (over y_hi, core), vocab: 32 (over x, z, y_lo).
Axes of the slice: x: 4, y: 4 (y_hi: 2, y_lo: 2; y = y_hi * 2 + y_lo), z: 4, core: 2. Of those that a mesh axis runs over, the one named last changes fastest.
Arguments:
- hidden_states: bfloat16 [256, 8192], P(('dp', 'vocab')), may hold values from -8 to 8
- head_weight: bfloat16 [8192, 65536], P(None, ('dp', 'vocab')), may hold values from -2 to 2
- teacher_codes: bfloat16 [256, 65536], P(('dp', 'vocab')), may hold values from -448 to 448, as said below
- teacher_scales: bfloat16 [256, 512], P(('dp', 'vocab')), may hold values from 0.5 to 1.5
- targets: int32 [256], replicated, may hold values from 0 to 65535
Outputs:
- hidden_grad: float32 [256, 8192], P(('dp', 'vocab'))
- head_grad: bfloat16 [8192, 65536], P(None, ('dp', 'vocab'))
- token_loss: float32 [256], replicated
Inputs may be any that keep to these rules, and one draw needn't show every extreme that they name: `teacher_codes`: codes lie within the range of an 8-bit float.
All inputs are finite; a program needn't handle non-finite values.
Results may differ from a plain program's by a relative error of at most 0.0041.
Values may be sent and summed in bfloat16 or wider, within the bound.
A program may use at most 128 MiB of HBM per device.

v0:
```python
import jax
import jax.numpy as jnp
from jax import lax
from jax.sharding import PartitionSpec as P

GRAD_SCALE = 32.0
CE_WEIGHT = 0.5


def dequantize(teacher_code, teacher_scale):
    token_count, width = teacher_code.shape
    block_count = teacher_scale.shape[1]
    blocked = teacher_code.astype(jnp.float32).reshape(
        token_count, block_count, width // block_count
    )
    return (blocked * teacher_scale.astype(jnp.float32)[:, :, None]).reshape(token_count, width)


def per_device(hidden_states, head_weight, teacher_codes, teacher_scales, targets):
    width_dev = head_weight.shape[1]
    teacher_code, teacher_scale = (
        lax.all_to_all(teacher_codes, ("dp", "vocab"), split_axis=1, concat_axis=0, tiled=True),
        lax.all_to_all(teacher_scales, ("dp", "vocab"), split_axis=1, concat_axis=0, tiled=True),
    )
    teacher = dequantize(teacher_code, teacher_scale)
    gathered = lax.all_gather(hidden_states, ("dp", "vocab"), axis=0, tiled=True)
    logits = jnp.dot(gathered, head_weight, preferred_element_type=jnp.float32)
    first_column = lax.axis_index(("dp", "vocab")) * width_dev
    columns = first_column + lax.broadcasted_iota(jnp.int32, (1, width_dev), 1)
    target_hit = (columns == targets[:, None]).astype(jnp.float32)
    target_local = jnp.sum(target_hit * logits, axis=1)
    peak_student, peak_teacher = lax.pmax(
        (jnp.max(logits, axis=1), jnp.max(teacher, axis=1)), ("dp", "vocab")
    )
    weight_student = jnp.exp(logits - peak_student[:, None])
    weight_teacher = jnp.exp(teacher - peak_teacher[:, None])
    total_student, total_teacher, cross_total, target_logit = lax.psum(
        (
            jnp.sum(weight_student, axis=1),
            jnp.sum(weight_teacher, axis=1),
            jnp.sum(weight_teacher * (teacher - logits), axis=1),
            target_local,
        ),
        ("dp", "vocab"),
    )
    log_student = peak_student + jnp.log(total_student)
    log_teacher = peak_teacher + jnp.log(total_teacher)
    token_loss = (
        cross_total / total_teacher
        - log_teacher
        + log_student
        + CE_WEIGHT * (log_student - target_logit)
    )
    student_prob = jnp.exp(logits - log_student[:, None])
    teacher_prob = jnp.exp(teacher - log_teacher[:, None])
    grad_logits = (
        GRAD_SCALE * ((1.0 + CE_WEIGHT) * student_prob - teacher_prob - CE_WEIGHT * target_hit)
    ).astype(jnp.bfloat16)
    head_grad = jnp.einsum(
        "td,tv->dv", gathered, grad_logits, preferred_element_type=jnp.float32
    ).astype(jnp.bfloat16)
    partial_value = jnp.einsum(
        "tv,dv->td", grad_logits, head_weight, preferred_element_type=jnp.float32
    )
    hidden_grad = lax.psum_scatter(partial_value, ("dp", "vocab"), scatter_dimension=0, tiled=True)
    return (hidden_grad, head_grad, token_loss)


def solution(mesh):
    return jax.shard_map(
        per_device,
        mesh=mesh,
        in_specs=(
            P(("dp", "vocab"), None),
            P(None, ("dp", "vocab")),
            P(("dp", "vocab"), None),
            P(("dp", "vocab"), None),
            P(),
        ),
        out_specs=(P(("dp", "vocab"), None), P(None, ("dp", "vocab")), P()),
        check_vma=False,
    )
```

profile of v0, /device:TPU:1, one launch (start us, length us, event | category | flops | bytes accessed | tf_op | source)
XLA Modules:
  0.0 639.3 jit_solution(15912636651673931413)
XLA Ops:
  7.2 0.0 all-gather.3.cloned.1.call-start
  7.2 0.7 all-gather.3.cloned.1.call-update
  7.9 0.8 all_to_all.22
  8.7 0.1 copy.14
  8.8 20.9 %all_to_all.26 = bf16[2,128,4]{2,0,1:T(2,128)(2,1)S(1)} all-to-all(bf16[2,128,4]{2,0,1:T(2,128)(2,1)S(1)} %copy.14), channel_id=1, replica_groups=mesh['dp'=4,'vocab'=32] {'dp','vocab'}, dimensions={1} | all-to-all | bytes 4096 | tf_op jit(solution)/shard_map/all_to_all | solution.py:23
  29.7 4.5 all-to-all-start
  34.2 0.0 all-reduce.5.cloned.1.call-start
  34.4 0.3 mul.57
  34.7 0.4 mul.60
  35.1 10.3 %all-to-all-done = bf16[2,128,512]{2,0,1:T(2,128)(2,1)S(1)} async-done(((bf16[2,128,512]{2,0,1:T(2,128)(2,1)}), bf16[2,128,512]{2,0,1:T(2,128)(2,1)S(1)}, u32[]{:S(2)}, u32[]{:S(2)}) %all-to-all-start) | async-done | bytes 262176 | tf_op jit(solution)/shard_map/all_to_all | solution.py:22
  45.3 0.3 fusion.6
  45.7 0.1 reduce_max.22
  45.8 0.2 convert_bitcast_fusion
  46.0 0.4 reshape.48
  46.4 271.9 %all-gather.3.cloned.1.call-done = bf16[128,2,8192]{2,1,0:T(2,128)(2,1)} async-done(((bf16[1,2,8192]{2,1,0:T(2,128)(2,1)}), bf16[128,2,8192]{2,1,0:T(2,128)(2,1)}) %all-gather.3.cloned.1.call-update) | async-done | bytes 4194320 | tf_op jit(solution)/shard_map/all_gather | solution.py:26
  318.3 7.2 %reshape.51 = bf16[256,8192]{1,0:T(8,128)(2,1)} reshape(bf16[128,2,8192]{2,1,0:T(2,128)(2,1)} %all-gather.3.cloned.1.call-done) | data formatting | bytes 8388608
  325.4 0.0 copy-start
  325.5 7.1 %fusion.7 = (f32[256]{0:T(256)S(1)}, f32[256,512]{1,0:T(8,128)S(1)}) fusion(bf16[256,8192]{1,0:T(8,128)(2,1)} %reshape.51, bf16[8192,512]{1,0:T(8,128)(2,1)} %param.6), kind=kOutput, calls=%fused_computation.20 | convolution fusion | flops 2147614464 | bytes 13108224 | tf_op jit(solution)/shard_map/dot_general | solution.py:27
  332.5 65.4 %all-reduce.2 = (f32[256]{0:T(256)S(1)}, f32[256]{0:T(256)S(1)}) all-reduce(f32[256]{0:T(256)S(1)} %reduce_max.22, f32[256]{0:T(256)S(1)} %get-tuple-element.24), channel_id=1, replica_groups=mesh['dp'=4,'vocab'=32] {'dp','vocab'}, use_global_device_ids=true, to_apply=%region_5.0 | all-reduce | flops 512 | bytes 4096 | tf_op jit(solution)/shard_map/pmax | solution.py:32
  397.9 0.1 sub.59
  398.1 0.6 exponential_reduce_fusion
  398.7 0.1 reduce_sum.40
  398.8 0.0 copy-done
  398.8 0.5 multiply_reduce_fusion
  399.3 63.1 %all-reduce.1 = (f32[256]{0:T(256)S(1)}, f32[256]{0:T(256)S(1)}, f32[256]{0:T(256)S(1)}, f32[256]{0:T(256)S(1)}) all-reduce(f32[256]{0:T(256)S(1)} %reduce_sum.40, f32[256]{0:T(256)S(1)} %get-tuple-element.14, f32[256]{0:T(256)S(1)} %get-tuple-element.13, f32[256]{0:T(256)S(1)} %get-tuple-element.12), channel_id=1, replica_groups=mesh['dp'=4,'vocab'=32] {'dp','vocab'}, use_global_device_ids=true, to_apply=%region_7.0 | all-reduce | flops 1024 | bytes 8192 | tf_op jit(solution)/shard_map/psum | solution.py:37
  462.4 0.6 multiply_add_fusion
  462.9 0.3 fusion.3
  463.2 9.0 %fusion.8 = f32[256,8192]{1,0:T(8,128)} fusion(bf16[256,512]{1,0:T(8,128)(2,1)S(1)} %fusion.3, bf16[8192,512]{1,0:T(8,128)(2,1)} %param.6), kind=kOutput, calls=%fused_computation.21 | convolution fusion | flops 2147483648 | bytes 17039360 | tf_op jit(solution)/shard_map/tv,dv->td/dot_general | solution.py:62
  472.2 0.0 all-reduce.5.cloned.1.call-update
  472.2 8.1 %fusion = bf16[8192,512]{0,1:T(8,128)(2,1)} fusion(bf16[256,512]{1,0:T(8,128)(2,1)S(1)} %fusion.3, bf16[256,8192]{1,0:T(8,128)(2,1)} %reshape.51), kind=kOutput, calls=%fused_computation.1 | convolution fusion | flops 2151677952 | bytes 12845056 | tf_op jit(solution)/shard_map/td,tv->dv/dot_general | solution.py:59
  480.3 12.0 %copy.15 = bf16[8192,512]{1,0:T(8,128)(2,1)} copy(bf16[8192,512]{0,1:T(8,128)(2,1)} %fusion) | data formatting | bytes 16777216
  492.3 138.5 %all-reduce.5.cloned.1.call-done = f32[256,8192]{1,0:T(8,128)} async-done(((f32[256,8192]{1,0:T(8,128)}), f32[256,8192]{1,0:T(8,128)}) %all-reduce.5.cloned.1.call-update) | async-done | bytes 8388624
  630.8 1.6 constant_dynamic-slice_fusion
  (2 shorter events, 0.1 us)
Async XLA Ops:
  7.2 311.1 %all-gather.3.cloned.1.call-start = ((), (), s32[]{:S(2)}) async-start(), calls=%async_computation.2 | async-start | bytes 4227072 | tf_op jit(solution)/shard_map/all_gather | solution.py:26
  29.7 15.6 %all-to-all-start = ((bf16[2,128,512]{2,0,1:T(2,128)(2,1)}), bf16[2,128,512]{2,0,1:T(2,128)(2,1)S(1)}, u32[]{:S(2)}, u32[]{:S(2)}) async-start(bf16[2,128,512]{2,0,1:T(2,128)(2,1)} %bitcast.31), calls=%async_computation | async-start | bytes 524288 | tf_op jit(solution)/shard_map/all_to_all | solution.py:22
  34.2 596.6 %all-reduce.5.cloned.1.call-start = ((), (), s32[]{:S(2)}) async-start(), calls=%async_computation.3 | async-start | bytes 16777216
  325.4 73.4 %copy-start = (s32[256]{0:T(256)S(1)}, s32[256]{0:T(256)}, u32[]{:S(2)}) copy-start(s32[256]{0:T(256)} %param.9) | copy-start | bytes 3076
Sparse Core Ops, SparseCore 0:
  9.7 308.5 all-gather.2
  472.4 158.4 all-reduce.4
where the time goes:
time: 640 us; the launch traced here: 639 us
  waiting for transfers between devices  421 us (66%)
  blocking collectives  149 us (23%)
  matrix products  24.1 us (4%)
  local copies, waits for them, and re-layouts  23.2 us (4%)
  between operations  14.1 us (2%)
    all_gather x1, waiting for transfers between devices, per_device(): lax.all_gather(hidden_states, ('dp', 'vocab'), axis=0, tiled=True)  272 us
    unnamed x3, waiting for transfers between devices  139 us
    pmax x1, blocking collectives, per_device(): lax.pmax((jnp.max(logits, axis=1), jnp.max(teacher, axis=1)), ('dp', 'voc...  65.4 us
    psum x1, blocking collectives, per_device(): lax.psum((jnp.sum(weight_student, axis=1), jnp.sum(weight_teacher, axis=1...  63.1 us
    all_to_all x1, blocking collectives, per_device(): lax.all_to_all(teacher_scales, ('dp', 'vocab'), split_axis=1, concat_axis...  20.9 us
    unnamed x5, local copies, waits for them, and re-layouts  20.8 us
  transfers between devices with their start and end apart: 3, of which 3 were waited for; matrix products, arithmetic and copies ran while one was open for 3% of the time, Pallas kernels for 0%

commit v1 on v0

v1 whole, which is shorter than its diff:
```python
import functools

import jax
import jax.numpy as jnp
from jax import lax
from jax.experimental import pallas as pl
from jax.experimental.pallas import tpu as pltpu
from jax.sharding import PartitionSpec as P

GRAD_SCALE = 32.0
CE_WEIGHT = 0.5
F32, BF16 = jnp.float32, jnp.bfloat16
MESH = pl.DeviceIdType.MESH
AXES = ("dp", "vocab")

CHUNK = 1024
WIDE = CHUNK + 128
PARTS = (
    (0, 384, 384, "xyz"),
    (384, 384, 384, "yzx"),
    (768, 384, 256, "zxy"),
)


def kernel(
    h_in, w_in, codes_in, scales_in, tgt_in,
    hg_out, loss_out, grad_out, h_out,
    h_all, w_all, src8, pre8, t1, t2, t3, t4, logits, teacher,
    st_core, st_x, st_y, st_z,
    own, send_c, recv_c, summed,
    r3a, r3b, r3c, f2a, f2b, f2c, b2a, b2b, b2c, r2a, r2b, r2c,
    f1a, f1b, f1c, r1a, r1b, r1c, fin_s, fin_r,
    send_sems, recv_sems, local_sems,
):
    dp, vo = lax.axis_index("dp"), lax.axis_index("vocab")
    me = {"x": vo // 8, "z": (vo // 2) % 4, "y": (dp // 2) * 2 + vo % 2, "c": dp % 2}

    def device(**other):
        at = {**me, **other}
        return ((at["y"] // 2) * 2 + at["c"], (at["x"] * 4 + at["z"]) * 2 + at["y"] % 2)

    def step(axis, k):
        return lax.rem(me[axis] + k, 2 if axis == "c" else 4)

    count = {"remote": 0, "local": 0}
    unsent = []

    def push(src, dst, **other):
        n = count["remote"]
        count["remote"] += 1
        copy = pltpu.make_async_remote_copy(
            src_ref=src, dst_ref=dst, send_sem=send_sems.at[n], recv_sem=recv_sems.at[n],
            device_id=device(**other), device_id_type=MESH,
        )
        copy.start()
        unsent.append(copy)
        return copy

    def local(src, dst):
        n = count["local"]
        count["local"] += 1
        copy = pltpu.make_async_copy(src, dst, local_sems.at[n])
        copy.start()
        return copy

    heads = []
    for c in range(2):
        for z in range(4):
            g = c * 4 + z
            heads.append(local(h_in.at[:, pl.ds(g * CHUNK, CHUNK)], src8.at[c, z, :, pl.ds(0, CHUNK)]))
            heads.append(local(scales_in.at[:, pl.ds(z * 128, 128)], src8.at[c, z, :, pl.ds(CHUNK, 128)]))
    own_codes = local(codes_in.at[:, :, me["x"]], t1.at[me["x"]])
    w_copy = local(w_in, w_all)

    barrier = pltpu.get_barrier_semaphore()
    partners = [dict(x=step("x", k)) for k in (1, 2, 3)] + [dict(y=step("y", k)) for k in (1, 2, 3)]
    partners += [dict(z=step("z", k), c=step("c", e)) for k in range(4) for e in range(2) if (k, e) != (0, 0)]
    for other in partners:
        pl.semaphore_signal(barrier, inc=1, device_id=device(**other), device_id_type=MESH)
    for copy in heads:
        copy.wait()
    pl.semaphore_wait(barrier, len(partners))

    arriving = []
    for k in range(4):
        for e in range(2):
            if (k, e) != (0, 0):
                z, c = step("z", k), step("c", e)
                arriving.append(push(src8.at[c, z], pre8.at[me["c"], me["z"]], z=z, c=c))
    pre8[me["c"], me["z"]] = src8[me["c"], me["z"]]
    for copy in arriving:
        copy.wait_recv()
    h_all[me["c"], me["z"], me["x"], me["y"]] = jnp.concatenate(
        [pre8[c, z].astype(F32) for z in range(4) for c in range(2)], axis=0
    ).astype(BF16)

    def gathered(part, free, **fixed):
        at = {**me, **fixed}
        index = [slice(None) if a in free else at[a] for a in "zxy"]
        return h_all.at[(me["c"], *index, slice(None), pl.ds(part[0], part[1]))]

    def gather_phase(part, p):
        order = part[3]
        view = gathered(part, order[:p])
        axis = order[p]
        return [push(view, view, **{axis: step(axis, k)}) for k in (1, 3, 2)]

    wave = [gather_phase(part, 0) for part in PARTS]
    codes_wave = [push(codes_in.at[:, :, step("x", k)], t1.at[me["x"]], x=step("x", k)) for k in (1, 3, 2)]
    for p in (1, 2):
        for i, part in enumerate(PARTS):
            for copy in wave[i]:
                copy.wait_recv()
            wave[i] = gather_phase(part, p)
        for copy in codes_wave:
            copy.wait_recv()
        if p == 1:
            own_codes.wait()
            codes_wave = [
                push(t1.at[:, step("y", k) // 2, :, :, step("y", k) % 2], t2.at[me["y"]], y=step("y", k))
                for k in (1, 3, 2)
            ]
            t2[me["y"]] = t1[:, me["y"] // 2, :, :, me["y"] % 2]
        else:
            codes_wave = [push(t2.at[:, :, :, step("z", k)], t3.at[me["z"]], z=step("z", k)) for k in (1, 3, 2)]
            t3[me["z"]] = t2[:, :, :, me["z"]]

    other_core = step("c", 1)
    crossing = []

    def cross(part, coordinate):
        view = gathered(part, part[3][:2], **{part[3][2]: coordinate})
        crossing.append(push(view, view, c=other_core))

    for part in PARTS:
        cross(part, me[part[3][2]])
    for n, k in enumerate((1, 3, 2)):
        for i, part in enumerate(PARTS):
            wave[i][n].wait_recv()
            cross(part, step(part[3][2], 4 - k))
    for copy in codes_wave:
        copy.wait_recv()
    codes_core = push(t3.at[:, :, :, other_core], t4.at[me["c"]], c=other_core)
    t4[me["c"]] = t3[:, :, :, me["c"]]

    w_copy.wait()
    logits[...] = jnp.zeros_like(logits)

    def add_logits(c):
        @pl.loop(0, 4)
        def _(z):
            rows = h_all[c, z, :, :, :, pl.ds(0, CHUNK)].reshape(256, CHUNK)
            logits[...] += jnp.dot(rows, w_all[c * 4 + z], preferred_element_type=F32)

    add_logits(me["c"])
    for copy in crossing:
        copy.wait_recv()
    add_logits(other_core)
    h_copy = local(h_all.at[:, :, :, :, :, pl.ds(0, CHUNK)], h_out)

    codes_core.wait_recv()
    block = lax.broadcasted_iota(jnp.int32, (128, 512), 0)
    column = lax.broadcasted_iota(jnp.int32, (128, 512), 1)
    pick = (block == vo * 4 + column // 128).astype(F32).astype(BF16)
    scale = jnp.dot(
        h_all[0, dp, :, :, :, pl.ds(CHUNK, 128)].reshape(256, 128), pick, preferred_element_type=F32
    )
    for x in range(4):
        for y in range(4):
            row = (x * 4 + y) * 16
            code = jnp.concatenate(
                [t4[c, z, y, x].astype(F32) for z in range(4) for c in range(2)], axis=0
            )
            teacher[pl.ds(row, 16), :] = code * scale[row : row + 16]

    lg, tc = logits[...], teacher[...]
    first = (dp * 32 + vo) * 512
    hit = (first + lax.broadcasted_iota(jnp.int32, (256, 512), 1)) == tgt_in[...]
    m_s = jnp.max(lg, axis=1, keepdims=True)
    m_t = jnp.max(tc, axis=1, keepdims=True)
    w_t = jnp.exp(tc - m_t)
    stats = (
        m_s, jnp.sum(jnp.exp(lg - m_s), axis=1, keepdims=True),
        m_t, jnp.sum(w_t, axis=1, keepdims=True),
        jnp.sum(w_t * (tc - lg), axis=1, keepdims=True),
        jnp.sum(jnp.where(hit, lg, 0.0), axis=1, keepdims=True),
    )
    lane = lax.broadcasted_iota(jnp.int32, (256, 128), 1)
    packed = jnp.zeros((256, 128), F32)
    for n, value in enumerate(stats):
        packed = jnp.where(lane == n, value, packed)
    mine = packed.T[:8]

    def merge(parts):
        m1 = functools.reduce(jnp.maximum, [p[0:1] for p in parts])
        m2 = functools.reduce(jnp.maximum, [p[2:3] for p in parts])
        e1 = [jnp.exp(p[0:1] - m1) for p in parts]
        e2 = [jnp.exp(p[2:3] - m2) for p in parts]
        s1 = sum(p[1:2] * e for p, e in zip(parts, e1))
        s2 = sum(p[3:4] * e for p, e in zip(parts, e2))
        cross_sum = sum(p[4:5] * e for p, e in zip(parts, e2))
        target = sum(p[5:6] for p in parts)
        pad = jnp.zeros((2, 256), F32)
        return jnp.concatenate([m1, s1, m2, s2, cross_sum, target, pad], axis=0)

    for axis, slots in (("c", st_core), ("x", st_x), ("y", st_y), ("z", st_z)):
        size = slots.shape[0]
        slots[0] = mine
        copies = [
            push(slots.at[0], slots.at[k], **{axis: step(axis, k)}) for k in ((1,) if size == 2 else (1, 3, 2))
        ]
        for copy in copies:
            copy.wait_recv()
        mine = merge([slots[k] for k in range(size)])

    log_s = mine[0:1] + jnp.log(mine[1:2])
    log_t = mine[2:3] + jnp.log(mine[3:4])
    loss = mine[4:5] / mine[3:4] - log_t + log_s + CE_WEIGHT * (log_s - mine[5:6])
    loss_out[...] = jnp.broadcast_to(loss, (8, 256))
    columns = jnp.concatenate([log_s, log_t, jnp.zeros((126, 256), F32)], axis=0).T
    grad = GRAD_SCALE * (
        (1.0 + CE_WEIGHT) * jnp.exp(logits[...] - columns[:, 0:1])
        - jnp.exp(teacher[...] - columns[:, 1:2])
        - CE_WEIGHT * hit.astype(F32)
    )
    grad_out[...] = grad.astype(BF16)

    def partial_of(c, z):
        return lax.dot_general(
            grad_out[...], w_all[c * 4 + z], (((1,), (1,)), ((), ())), preferred_element_type=F32
        ).reshape(4, 4, 16, CHUNK)

    crossing = []
    for z in range(4):
        send_c[z] = partial_of(other_core, z).astype(BF16)
        crossing.append(push(send_c.at[z], recv_c.at[z], c=other_core))

    @pl.loop(0, 4)
    def _(z):
        own[z] = partial_of(me["c"], z)

    for copy in crossing:
        copy.wait_recv()

    @pl.loop(0, 4)
    def _(z):
        total = own[z] + recv_c[z].astype(F32)
        own[z] = total
        summed[z] = total.astype(BF16)

    r3, f2, b2 = (r3a, r3b, r3c), (f2a, f2b, f2c), (b2a, b2b, b2c)
    r2, f1, r1 = (r2a, r2b, r2c), (f1a, f1b, f1c), (r1a, r1b, r1c)

    def at_axis(axes, axis, coordinate):
        return tuple(coordinate if a == axis else slice(None) for a in axes)

    waves = []
    for i, part in enumerate(PARTS):
        axis, cols = part[3][2], pl.ds(part[0], part[2])
        waves.append([
            push(summed.at[(*at_axis("zxy", axis, step(axis, k)), slice(None), cols)], r3[i].at[k - 1], **{axis: step(axis, k)})
            for k in (1, 3, 2)
        ])
    for i, part in enumerate(PARTS):
        axis, cols = part[3][2], pl.ds(part[0], part[2])
        for copy in waves[i]:
            copy.wait_recv()
        total = own[(*at_axis("zxy", axis, me[axis]), slice(None), cols)]
        for k in range(3):
            total = total + r3[i][k].astype(F32)
        f2[i][...] = total
        b2[i][...] = total.astype(BF16)
        rest = "zxy".replace(axis, "")
        axis = part[3][1]
        waves[i] = [
            push(b2[i].at[at_axis(rest, axis, step(axis, k))], r2[i].at[k - 1], **{axis: step(axis, k)})
            for k in (1, 3, 2)
        ]
    for i, part in enumerate(PARTS):
        for copy in waves[i]:
            copy.wait_recv()
        rest = "zxy".replace(part[3][2], "")
        axis = part[3][1]
        total = f2[i][at_axis(rest, axis, me[axis])]
        for k in range(3):
            total = total + r2[i][k].astype(F32)
        f1[i][...] = total
        axis = part[3][0]
        waves[i] = [push(f1[i].at[step(axis, k)], r1[i].at[k - 1], **{axis: step(axis, k)}) for k in (1, 3, 2)]
    for i, part in enumerate(PARTS):
        for copy in waves[i]:
            copy.wait_recv()
        total = f1[i][me[part[3][0]]]
        for k in range(3):
            total = total + r1[i][k]
        for z in range(4):
            for c in range(2):
                row = (z * 2 + c) * 2
                fin_s[c, z, :, pl.ds(part[0], part[2])] = total[row : row + 2]

    arriving = []
    for k in range(4):
        for e in range(2):
            if (k, e) != (0, 0):
                z, c = step("z", k), step("c", e)
                arriving.append(push(fin_s.at[c, z], fin_r.at[me["c"], me["z"]], z=z, c=c))
    fin_r[me["c"], me["z"]] = fin_s[me["c"], me["z"]]
    for copy in arriving:
        copy.wait_recv()
    for c in range(2):
        for z in range(4):
            hg_out[:, pl.ds((c * 4 + z) * CHUNK, CHUNK)] = fin_r[c, z]

    h_copy.wait()
    for copy in unsent:
        copy.wait_send()


def head_kernel(h_ref, grad_ref, out_ref):
    out_ref[...] = lax.dot_general(
        h_ref[0], grad_ref[...], (((0,), (0,)), ((), ())), preferred_element_type=F32
    ).astype(BF16)


def per_device(hidden_states, head_weight, teacher_codes, teacher_scales, targets):
    codes = teacher_codes.reshape(2, 128, 512).transpose(1, 0, 2).reshape(2, 2, 4, 4, 2, 2, 512)
    weight = head_weight.reshape(8, CHUNK, 512)
    target = targets.reshape(2, 2, 4, 4, 2, 2).transpose(2, 0, 4, 3, 1, 5).reshape(256, 1)

    vmem = pltpu.VMEM
    scratch = [
        vmem((2, 4, 4, 4, 16, WIDE), BF16),
        vmem((8, CHUNK, 512), BF16),
        vmem((2, 4, 2, WIDE), BF16),
        vmem((2, 4, 2, WIDE), BF16),
        vmem((4, 2, 2, 4, 2, 2, 512), BF16),
        vmem((4, 4, 2, 4, 2, 512), BF16),
        vmem((4, 4, 4, 2, 2, 512), BF16),
        vmem((2, 4, 4, 4, 2, 512), BF16),
        vmem((256, 512), F32),
        vmem((256, 512), F32),
        vmem((2, 8, 256), F32),
        vmem((4, 8, 256), F32),
        vmem((4, 8, 256), F32),
        vmem((4, 8, 256), F32),
        vmem((4, 4, 4, 16, CHUNK), F32),
        vmem((4, 4, 4, 16, CHUNK), BF16),
        vmem((4, 4, 4, 16, CHUNK), BF16),
        vmem((4, 4, 4, 16, CHUNK), BF16),
    ]
    widths = [part[2] for part in PARTS]
    scratch += [vmem((3, 4, 4, 16, n), BF16) for n in widths]
    scratch += [vmem((4, 4, 16, n), F32) for n in widths]
    scratch += [vmem((4, 4, 16, n), BF16) for n in widths]
    scratch += [vmem((3, 4, 16, n), BF16) for n in widths]
    scratch += [vmem((4, 16, n), F32) for n in widths]
    scratch += [vmem((3, 16, n), F32) for n in widths]
    scratch += [vmem((2, 4, 2, CHUNK), F32), vmem((2, 4, 2, CHUNK), F32)]
    scratch += [
        pltpu.SemaphoreType.DMA((112,)),
        pltpu.SemaphoreType.DMA((112,)),
        pltpu.SemaphoreType.DMA((20,)),
    ]
    hidden_grad, loss, grad, gathered = pl.pallas_call(
        kernel,
        out_shape=(
            jax.ShapeDtypeStruct((2, 8192), F32),
            jax.ShapeDtypeStruct((8, 256), F32),
            jax.ShapeDtypeStruct((256, 512), BF16),
            jax.ShapeDtypeStruct((2, 4, 4, 4, 16, CHUNK), BF16),
        ),
        in_specs=[pl.BlockSpec(memory_space=pl.ANY)] * 4 + [pl.BlockSpec(memory_space=pltpu.VMEM)],
        out_specs=[pl.BlockSpec(memory_space=pltpu.VMEM)] * 3 + [pl.BlockSpec(memory_space=pl.ANY)],
        scratch_shapes=scratch,
        compiler_params=pltpu.CompilerParams(
            collective_id=0, has_side_effects=True, vmem_limit_bytes=56 * 1024 * 1024
        ),
    )(hidden_states, weight, codes, teacher_scales, target)

    head_grad = pl.pallas_call(
        head_kernel,
        grid=(8,),
        out_shape=jax.ShapeDtypeStruct((8192, 512), BF16),
        in_specs=[
            pl.BlockSpec((1, 256, CHUNK), lambda g: (g, 0, 0)),
            pl.BlockSpec((256, 512), lambda g: (0, 0)),
        ],
        out_specs=pl.BlockSpec((CHUNK, 512), lambda g: (g, 0)),
        compiler_params=pltpu.CompilerParams(vmem_limit_bytes=32 * 1024 * 1024),
    )(gathered.reshape(8, 256, CHUNK), grad)

    token_loss = loss[0].reshape(4, 2, 2, 4, 2, 2).transpose(1, 4, 0, 3, 2, 5).reshape(256)
    return hidden_grad, head_grad, token_loss


def solution(mesh):
    return jax.shard_map(
        per_device,
        mesh=mesh,
        in_specs=(
            P(AXES, None),
            P(None, AXES),
            P(AXES, None),
            P(AXES, None),
            P(),
        ),
        out_specs=(P(AXES, None), P(None, AXES), P()),
        check_vma=False,
    )
```

time: 640 us -> 93.3 us (0.15)
  waiting for transfers between devices: 421 us -> 0 us
  blocking collectives: 149 us -> 0 us
  Pallas kernels: 0 us -> 85.3 us
  matrix products: 24.1 us -> 0 us
  local copies, waits for them, and re-layouts: 23.2 us -> 7.11 us
  between operations: 14.1 us -> 0.68 us
    all_gather x1 -> x0, waiting for transfers between devices: 272 us -> none  [per_device(): lax.all_gather(hidden_states, ('dp', 'vocab'), axis=0, tiled=True)]
    unnamed x3 -> x0, waiting for transfers between devices: 139 us -> none
    pallas_call x0 -> x2, Pallas kernels: none -> 85.3 us  [the longest x1 79 us: per_device(): pl.pallas_call(kernel, out_shape=(jax.ShapeDtypeStruct((2, 8192), F32), j...]
    pmax x1 -> x0, blocking collectives: 65.4 us -> none  [per_device(): lax.pmax((jnp.max(logits, axis=1), jnp.max(teacher, axis=1)), ('dp', 'voc...]
    psum x1 -> x0, blocking collectives: 63.1 us -> none  [per_device(): lax.psum((jnp.sum(weight_student, axis=1), jnp.sum(weight_teacher, axis=1...]
    dot_general x3 -> x0, matrix products: 24.1 us -> none  [the longest x1 8.97 us: per_device(): jnp.einsum('tv,dv->td', grad_logits, head_weight, preferred_element_type=...]
    all_to_all x1 -> x0, blocking collectives: 20.9 us -> none  [per_device(): lax.all_to_all(teacher_scales, ('dp', 'vocab'), split_axis=1, concat_axis...]
    unnamed x5 -> x7, local copies, waits for them, and re-layouts: 20.8 us -> 3.77 us
  transfers between devices with their start and end apart: 3 -> 0, of which waited for: 3 -> 0; matrix products, arithmetic and copies ran while one was open for 3% -> 0% of each run, Pallas kernels for 0% -> 0%
where the time goes in v1:
time: 93.3 us; the launch traced here: 93.1 us
  Pallas kernels  85.3 us (91%)
  local copies, waits for them, and re-layouts  7.11 us (8%)
    pallas_call x1, Pallas kernels, per_device(): pl.pallas_call(kernel, out_shape=(jax.ShapeDtypeStruct((2, 8192), F32), j...  79 us
    pallas_call x1, Pallas kernels, per_device(): pl.pallas_call(head_kernel, grid=(8,), out_shape=jax.ShapeDtypeStruct((81...  6.26 us
    unnamed x7, local copies, waits for them, and re-layouts  3.77 us

profile of v1, /device:TPU:1, one launch (start us, length us, event | category | flops | bytes accessed | tf_op | source)
XLA Modules:
  0.0 93.1 jit_solution(14387973730309799811)
XLA Ops:
  0.6 0.8 reshape.30
  1.5 0.1 copy.10
  1.5 0.8 reshape.34.tgt_in
  2.3 79.0 %shard_map.76 = (f32[2,8192]{1,0:T(2,128)}, f32[8,256]{1,0:T(8,128)}, bf16[256,512]{1,0:T(8,128)(2,1)}, bf16[2,4,4,4,16,1024]{5,4,3,2,1,0:T(8,128)(2,1)}) custom-call(bf16[2,8192]{1,0:T(2,128)(2,1)} %h_in.1, bf16[8,1024,512]{2,1,0:T(8,128)(2,1)} %bitcast.10, bf16[2,2,4,4,2,2,512]{6,5,4,3,2,1,0:T(2,128)(2,1)} %bitcast.11, bf16[2,512]{1,0:T(2,128)(2,1)} %scales_in.1, ...), custom_call_target="tpu_custom_call" | custom-call | tf_op jit(solution)/shard_map/pallas_call | solution.py:364
  81.4 0.0 copy-start.2
  81.4 0.7 slice_reduce_fusion
  82.1 0.2 reshape_squeeze.3
  82.3 0.7 reshape.33
  83.1 0.0 copy-start
  83.1 2.2 %copy-done = bf16[2,4,4,4,16,1024]{5,4,3,2,1,0:T(8,128)(2,1)S(1)} copy-done((bf16[2,4,4,4,16,1024]{5,4,3,2,1,0:T(8,128)(2,1)S(1)}, bf16[2,4,4,4,16,1024]{5,4,3,2,1,0:T(8,128)(2,1)}, u32[]{:S(2)}) %copy-start) | copy-done | bytes 4194328
  85.2 0.0 copy-start.1
  85.2 0.9 %copy-done.1 = bf16[256,512]{1,0:T(8,128)(2,1)S(1)} copy-done((bf16[256,512]{1,0:T(8,128)(2,1)S(1)}, bf16[256,512]{1,0:T(8,128)(2,1)}, u32[]{:S(2)}) %copy-start.1) | copy-done | bytes 262168
  86.2 6.3 %shard_map.77 = bf16[8192,512]{1,0:T(8,128)(2,1)} custom-call(bf16[8,256,1024]{2,1,0:T(8,128)(2,1)S(1)} %bitcast.9, bf16[256,512]{1,0:T(8,128)(2,1)S(1)} %copy-done.1), custom_call_target="tpu_custom_call" | custom-call | tf_op jit(solution)/shard_map/pallas_call | solution.py:380
  92.5 0.0 copy-done.2
  92.5 0.6 copy.14
  (1 shorter events, 0.0 us)
Async XLA Ops:
  81.4 11.1 %copy-start.2 = (f32[2,8192]{1,0:T(2,128)S(1)}, f32[2,8192]{1,0:T(2,128)}, u32[]{:S(2)}) copy-start(f32[2,8192]{1,0:T(2,128)} %get-tuple-element.14) | copy-start | bytes 196612
  83.1 2.2 %copy-start = (bf16[2,4,4,4,16,1024]{5,4,3,2,1,0:T(8,128)(2,1)S(1)}, bf16[2,4,4,4,16,1024]{5,4,3,2,1,0:T(8,128)(2,1)}, u32[]{:S(2)}) copy-start(bf16[2,4,4,4,16,1024]{5,4,3,2,1,0:T(8,128)(2,1)} %get-tuple-element.8) | copy-start | bytes 12582916
  85.2 0.9 %copy-start.1 = (bf16[256,512]{1,0:T(8,128)(2,1)S(1)}, bf16[256,512]{1,0:T(8,128)(2,1)}, u32[]{:S(2)}) copy-start(bf16[256,512]{1,0:T(8,128)(2,1)} %get-tuple-element.9.grad_ref) | copy-start | bytes 786436

commit v2 on v1

v2 whole, which is shorter than its diff:
```python
import functools

import jax
import jax.numpy as jnp
from jax import lax
from jax.experimental import pallas as pl
from jax.experimental.pallas import tpu as pltpu
from jax.sharding import PartitionSpec as P

GRAD_SCALE = 32.0
CE_WEIGHT = 0.5
F32, BF16 = jnp.float32, jnp.bfloat16
MESH = pl.DeviceIdType.MESH
AXES = ("dp", "vocab")

CHUNK = 1024
WIDE = CHUNK + 128
PARTS = (
    (0, 384, 384, "xyz"),
    (384, 384, 384, "yzx"),
    (768, 384, 256, "zxy"),
)


Z_ORDER = (2, 1, 3, 0)


def kernel(
    h_in, w_in, codes_in, scales_in, tgt_in,
    hg_out, loss_out, grad_out, ht_out,
    h_all, w_all, src8, pre8, t1, t2, t3, t4, logits, teacher, grad_v, ht_v,
    st_a, st_b, own, send_c, recv_c, summed,
    fl_a, fl_b, fl_c, fr_a, fr_b, fr_c, rl_a, rl_b, rl_c, rr_a, rr_b, rr_c,
    f2a, f2b, f2c, b2a, b2b, b2c, r2a, r2b, r2c,
    f1a, f1b, f1c, r1a, r1b, r1c, fin_s, fin_r, loss_v,
    send_sems, recv_sems, local_sems,
):
    dp, vo = lax.axis_index("dp"), lax.axis_index("vocab")
    me = {"x": vo // 8, "z": (vo // 2) % 4, "y": (dp // 2) * 2 + vo % 2, "c": dp % 2}

    def device(**other):
        at = {**me, **other}
        return ((at["y"] // 2) * 2 + at["c"], (at["x"] * 4 + at["z"]) * 2 + at["y"] % 2)

    def step(axis, k):
        return lax.rem(me[axis] + k, 2 if axis == "c" else 4)

    count = {"remote": 0, "local": 0}
    unsent, unstored = [], []

    def push(src, dst, **other):
        n = count["remote"]
        count["remote"] += 1
        copy = pltpu.make_async_remote_copy(
            src_ref=src, dst_ref=dst, send_sem=send_sems.at[n], recv_sem=recv_sems.at[n],
            device_id=device(**other), device_id_type=MESH,
        )
        copy.start()
        unsent.append(copy)
        return copy

    def local(src, dst):
        n = count["local"]
        count["local"] += 1
        copy = pltpu.make_async_copy(src, dst, local_sems.at[n])
        copy.start()
        return copy

    barrier = pltpu.get_barrier_semaphore()
    partners = [dict(x=step("x", i), y=step("y", k)) for i in range(4) for k in range(4) if (i, k) != (0, 0)]
    group = [(k, e) for k in range(4) for e in range(2) if (k, e) != (0, 0)]
    partners += [dict(z=step("z", k), c=step("c", e)) for k, e in group]
    for other in partners:
        pl.semaphore_signal(barrier, inc=1, device_id=device(**other), device_id_type=MESH)

    heads = [local(h_in, src8.at[:, :, :, pl.ds(0, CHUNK)])]
    heads += [local(scales_in, src8.at[c, :, :, pl.ds(CHUNK, 128)]) for c in range(2)]
    own_codes = local(codes_in.at[:, :, me["x"]], t1.at[me["x"]])
    w_copy = local(w_in, w_all)
    for copy in heads:
        copy.wait()
    pl.semaphore_wait(barrier, len(partners))

    arriving = []
    for k, e in group:
        z, c = step("z", k), step("c", e)
        arriving.append(push(src8.at[c, z], pre8.at[me["c"], me["z"]], z=z, c=c))
    pre8[me["c"], me["z"]] = src8[me["c"], me["z"]]
    k_row = lax.broadcasted_iota(jnp.int32, (256, 256), 0)
    n_col = lax.broadcasted_iota(jnp.int32, (256, 256), 1)
    natural = (
        ((k_row >> 5) & 1) * 128 + ((k_row >> 1) & 1) * 64 + (k_row >> 6) * 16
        + ((k_row >> 2) & 3) * 4 + ((k_row >> 4) & 1) * 2 + (k_row & 1)
    )
    reorder = natural == n_col
    target = jnp.sum(jnp.where(reorder, tgt_in[...].astype(F32), 0.0), axis=1, keepdims=True)
    first = (dp * 32 + vo) * 512
    hit = (first + lax.broadcasted_iota(jnp.int32, (256, 512), 1)).astype(F32) == target
    for copy in arriving:
        copy.wait_recv()
    h_all[me["c"], me["z"], me["x"], me["y"]] = jnp.concatenate(
        [pre8[c, z].astype(F32) for z in range(4) for c in range(2)], axis=0
    ).astype(BF16)

    def gathered(part, free, half=None, **fixed):
        at = {**me, **fixed}
        index, halved = [], half is None
        for a in "zxy":
            if a not in free:
                index.append(at[a])
            elif halved:
                index.append(slice(None))
            else:
                index.append(pl.ds(half * 2, 2))
                halved = True
        return h_all.at[(me["c"], *index, slice(None), pl.ds(part[0], part[1]))]

    def gather_phase(part, p):
        order = part[3]
        view = gathered(part, order[:p])
        axis = order[p]
        return [push(view, view, **{axis: step(axis, k)}) for k in (2, 1, 3)]

    wave = [gather_phase(part, 0) for part in PARTS]
    codes_wave = [push(codes_in.at[:, :, step("x", k)], t1.at[me["x"]], x=step("x", k)) for k in (2, 1, 3)]
    for i, part in enumerate(PARTS):
        for copy in wave[i]:
            copy.wait_recv()
        wave[i] = gather_phase(part, 1)
    for copy in codes_wave:
        copy.wait_recv()
    own_codes.wait()
    codes_wave = [
        push(t1.at[:, step("y", k) // 2, :, :, step("y", k) % 2], t2.at[me["y"]], y=step("y", k))
        for k in (2, 1, 3)
    ]
    t2[me["y"]] = t1[:, me["y"] // 2, :, :, me["y"] % 2]

    other_core = step("c", 1)
    crossing, right, left = [], [], []

    def ring(part, coordinate, half, k):
        axis = part[3][2]
        view = gathered(part, part[3][:2], half, **{axis: coordinate})
        return push(view, view, **{axis: step(axis, k)})

    def cross(part, coordinate, half=None):
        view = gathered(part, part[3][:2], half, **{part[3][2]: coordinate})
        crossing.append(push(view, view, c=other_core))

    for i, part in enumerate(PARTS):
        for copy in wave[i]:
            copy.wait_recv()
        here = me[part[3][2]]
        up0, down1 = ring(part, here, 0, 1), ring(part, here, 1, 3)
        right.append([up0, ring(part, here, 1, 1)])
        left.append([ring(part, here, 0, 3), down1])
    for part in PARTS:
        cross(part, me[part[3][2]])
    forward = []
    for i, part in enumerate(PARTS):
        right[i][0].wait_recv()
        up = ring(part, step(part[3][2], 3), 0, 1)
        left[i][1].wait_recv()
        forward.append((up, ring(part, step(part[3][2], 1), 1, 3)))
    for copy in codes_wave:
        copy.wait_recv()
    codes_wave = [push(t2.at[:, :, :, step("z", k)], t3.at[me["z"]], z=step("z", k)) for k in (2, 1, 3)]
    t3[me["z"]] = t2[:, :, :, me["z"]]
    for i, part in enumerate(PARTS):
        right[i][1].wait_recv()
        cross(part, step(part[3][2], 3))
        left[i][0].wait_recv()
        cross(part, step(part[3][2], 1))
    for i, part in enumerate(PARTS):
        forward[i][0].wait_recv()
        cross(part, step(part[3][2], 2), 0)
        forward[i][1].wait_recv()
        cross(part, step(part[3][2], 2), 1)
    for copy in codes_wave:
        copy.wait_recv()
    codes_core = push(t3.at[:, :, :, other_core], t4.at[me["c"]], c=other_core)
    t4[me["c"]] = t3[:, :, :, me["c"]]

    w_copy.wait()
    logits[...] = jnp.zeros_like(logits)

    def add_logits(c):
        @pl.loop(0, 4)
        def _(z):
            rows = h_all[c, z, :, :, :, pl.ds(0, CHUNK)].reshape(256, CHUNK)
            logits[...] += jnp.dot(rows, w_all[c * 4 + z], preferred_element_type=F32)

    add_logits(me["c"])
    block = lax.broadcasted_iota(jnp.int32, (128, 512), 0)
    column = lax.broadcasted_iota(jnp.int32, (128, 512), 1)
    pick = (block == vo * 4 + column // 128).astype(F32).astype(BF16)
    scale = jnp.dot(
        h_all[me["c"], dp, :, :, :, pl.ds(CHUNK, 128)].reshape(256, 128), pick, preferred_element_type=F32
    )
    codes_core.wait_recv()
    for x in range(4):
        for y in range(4):
            row = (x * 4 + y) * 16
            code = jnp.concatenate(
                [t4[c, z, y, x].astype(F32) for z in range(4) for c in range(2)], axis=0
            )
            teacher[pl.ds(row, 16), :] = code * scale[row : row + 16]
    for copy in crossing:
        copy.wait_recv()
    add_logits(other_core)

    lg, tc = logits[...], teacher[...]
    m_s = jnp.max(lg, axis=1, keepdims=True)
    m_t = jnp.max(tc, axis=1, keepdims=True)
    w_t = jnp.exp(tc - m_t)
    stats = (
        m_s, jnp.sum(jnp.exp(lg - m_s), axis=1, keepdims=True),
        m_t, jnp.sum(w_t, axis=1, keepdims=True),
        jnp.sum(w_t * (tc - lg), axis=1, keepdims=True),
        jnp.sum(jnp.where(hit, lg, 0.0), axis=1, keepdims=True),
    )
    lane = lax.broadcasted_iota(jnp.int32, (256, 128), 1)
    packed = jnp.zeros((256, 128), F32)
    for n, value in enumerate(stats):
        packed = jnp.where(lane == n, value, packed)
    mine = packed.T[:8]

    def merge(parts):
        m1 = functools.reduce(jnp.maximum, [p[0:1] for p in parts])
        m2 = functools.reduce(jnp.maximum, [p[2:3] for p in parts])
        e1 = [jnp.exp(p[0:1] - m1) for p in parts]
        e2 = [jnp.exp(p[2:3] - m2) for p in parts]
        s1 = sum(p[1:2] * e for p, e in zip(parts, e1))
        s2 = sum(p[3:4] * e for p, e in zip(parts, e2))
        cross_sum = sum(p[4:5] * e for p, e in zip(parts, e2))
        target = sum(p[5:6] for p in parts)
        pad = jnp.zeros((2, 256), F32)
        return jnp.concatenate([m1, s1, m2, s2, cross_sum, target, pad], axis=0)

    def transpose_chunks(c):
        @pl.loop(0, 4)
        def _(z):
            ht_v[c * 4 + z] = h_all[c, z, :, :, :, pl.ds(0, CHUNK)].reshape(256, CHUNK).T
        unstored.append(local(ht_v.at[pl.ds(c * 4, 4)], ht_out.at[pl.ds(c * 4, 4)]))

    st_a[0] = mine
    copies = [
        push(st_a.at[0], st_a.at[1 + n], z=step("z", k), c=step("c", e)) for n, (k, e) in enumerate(group)
    ]
    transpose_chunks(0)
    for copy in copies:
        copy.wait_recv()
    mine = merge([st_a[k] for k in range(8)])
    st_b[0] = mine
    pairs = [(i, k) for i in range(4) for k in range(4) if (i, k) != (0, 0)]
    copies = [
        push(st_b.at[0], st_b.at[1 + n], x=step("x", i), y=step("y", k)) for n, (i, k) in enumerate(pairs)
    ]
    transpose_chunks(1)
    for copy in copies:
        copy.wait_recv()
    mine = merge([st_b[k] for k in range(16)])

    log_s = mine[0:1] + jnp.log(mine[1:2])
    log_t = mine[2:3] + jnp.log(mine[3:4])
    loss = mine[4:5] / mine[3:4] - log_t + log_s + CE_WEIGHT * (log_s - mine[5:6])
    columns = jnp.concatenate([log_s, log_t, loss, jnp.zeros((125, 256), F32)], axis=0).T
    grad = GRAD_SCALE * (
        (1.0 + CE_WEIGHT) * jnp.exp(logits[...] - columns[:, 0:1])
        - jnp.exp(teacher[...] - columns[:, 1:2])
        - CE_WEIGHT * hit.astype(F32)
    )
    grad_v[...] = grad.astype(BF16)
    unstored.append(local(grad_v, grad_out))

    def partial_of(c, j):
        return lax.dot_general(
            grad_v[...], w_all[c * 4 + step("z", Z_ORDER[j])], (((1,), (1,)), ((), ())), preferred_element_type=F32
        ).reshape(4, 4, 16, CHUNK)

    crossing = []

    def send_partial(j):
        send_c[j] = partial_of(other_core, j).astype(BF16)
        crossing.append(push(send_c.at[j], recv_c.at[j], c=other_core))

    fl, fr, rl, rr = (fl_a, fl_b, fl_c), (fr_a, fr_b, fr_c), (rl_a, rl_b, rl_c), (rr_a, rr_b, rr_c)
    f2, b2 = (f2a, f2b, f2c), (b2a, b2b, b2c)
    r2, f1, r1 = (r2a, r2b, r2c), (f1a, f1b, f1c), (r1a, r1b, r1c)
    half0, half1 = two = pl.ds(0, 2), pl.ds(2, 2)
    ring_waits = {}

    def block_of(i, k, j, half):
        cols = pl.ds(PARTS[i][0], PARTS[i][2])
        if i == 0:
            return (Z_ORDER.index(k), slice(None), half, slice(None), cols)
        if i == 1:
            return (two[j], step("x", k), half, slice(None), cols)
        return (two[j], half, step("y", k), slice(None), cols)

    def landing(i, j, half):
        return (slice(None), half) if i == 0 else (j, slice(None), half)

    def ring_push(i, k, j, half, buffer, toward):
        axis = PARTS[i][3][2]
        if buffer is fl or buffer is fr:
            place = slice(None) if i == 0 else j
        else:
            place = landing(i, j, half)
        return push(
            summed.at[block_of(i, k, j, half)], buffer[i].at[place], **{axis: step(axis, toward)}
        )

    def ring_opposite(i, j):
        ring_waits[i, j] = [ring_push(i, 2, j, half0, fl, 1), ring_push(i, 2, j, half1, fr, 3)]

    def ring_up(i, j):
        ring_waits[i, j].append(ring_push(i, 1, j, half1, rl, 1))

    def ring_down(i, j):
        ring_waits[i, j].append(ring_push(i, 3, j, half0, rr, 3))

    def ring_forward(i, j):
        waits = ring_waits[i, j]
        place = slice(None) if i == 0 else j
        for n, (k, half, came, buffer) in enumerate(((1, half0, fl, rl), (3, half1, fr, rr))):
            waits[n].wait_recv()
            index = block_of(i, k, j, half)
            summed[index] = (own[index] + came[i][place].astype(F32)).astype(BF16)
            waits.append(ring_push(i, k, j, half, buffer, k))

    def add_chunk(j):
        crossing[j].wait_recv()
        total = own[j] + recv_c[j].astype(F32)
        own[j] = total
        summed[j] = total.astype(BF16)

    send_partial(0)
    send_partial(1)
    own[0] = partial_of(me["c"], 0)
    add_chunk(0)
    ring_opposite(0, 0)
    send_partial(2)
    own[1] = partial_of(me["c"], 1)
    add_chunk(1)
    ring_opposite(1, 0)
    ring_opposite(2, 0)
    ring_up(0, 0)
    for i in (1, 2):
        ring_up(i, 0)
        ring_down(i, 0)
    send_partial(3)
    own[2] = partial_of(me["c"], 2)
    add_chunk(2)
    ring_down(0, 0)
    ring_forward(0, 0)
    own[3] = partial_of(me["c"], 3)
    add_chunk(3)
    ring_opposite(1, 1)
    ring_opposite(2, 1)
    for i in (1, 2):
        ring_up(i, 1)
        ring_down(i, 1)
    ring_forward(1, 0)
    ring_forward(2, 0)
    ring_forward(1, 1)
    ring_forward(2, 1)

    def at_axis(axes, axis, coordinate):
        return tuple(coordinate if a == axis else slice(None) for a in axes)

    waves = [None] * 3
    for i, part in enumerate(PARTS):
        for j in range(1 if i == 0 else 2):
            for copy in ring_waits[i, j][2:]:
                copy.wait_recv()
        axis, cols = part[3][2], pl.ds(part[0], part[2])
        mine_at = 3 if axis == "z" else me[axis]
        total = own[(*at_axis("zxy", axis, mine_at), slice(None), cols)]
        total = total + rl[i][...].reshape(total.shape).astype(F32) + rr[i][...].reshape(total.shape).astype(F32)
        f2[i][...] = total
        b2[i][...] = total.astype(BF16)
        rest = "zxy".replace(axis, "")
        axis = part[3][1]
        waves[i] = [
            push(
                b2[i].at[at_axis(rest, axis, Z_ORDER.index(k) if axis == "z" else step(axis, k))],
                r2[i].at[k - 1], **{axis: step(axis, k)},
            )
            for k in (2, 1, 3)
        ]
    for i, part in enumerate(PARTS):
        for copy in waves[i]:
            copy.wait_recv()
        rest = "zxy".replace(part[3][2], "")
        axis = part[3][1]
        total = f2[i][at_axis(rest, axis, 3 if axis == "z" else me[axis])]
        for k in range(3):
            total = total + r2[i][k].astype(F32)
        f1[i][...] = total
        axis = part[3][0]
        waves[i] = [
            push(
                f1[i].at[Z_ORDER.index(k) if axis == "z" else step(axis, k)], r1[i].at[k - 1],
                **{axis: step(axis, k)},
            )
            for k in (2, 1, 3)
        ]
    loss_v[...] = jnp.broadcast_to(
        jnp.sum(jnp.where(reorder, columns[:, 2:3], 0.0), axis=0, keepdims=True), (8, 256)
    )
    unstored.append(local(loss_v, loss_out))
    for i, part in enumerate(PARTS):
        for copy in waves[i]:
            copy.wait_recv()
        total = f1[i][3 if part[3][0] == "z" else me[part[3][0]]]
        for k in range(3):
            total = total + r1[i][k]
        for z in range(4):
            for c in range(2):
                row = (z * 2 + c) * 2
                fin_s[c, z, :, pl.ds(part[0], part[2])] = total[row : row + 2]

    arriving = []
    for k, e in group:
        z, c = step("z", k), step("c", e)
        arriving.append(push(fin_s.at[c, z], fin_r.at[me["c"], me["z"]], z=z, c=c))
    fin_r[me["c"], me["z"]] = fin_s[me["c"], me["z"]]
    for copy in arriving:
        copy.wait_recv()
    unstored.append(local(fin_r, hg_out))
    for copy in unsent:
        copy.wait_send()
    for copy in unstored:
        copy.wait()


def head_kernel(ht_ref, grad_ref, hg_ref, loss_ref, out_ref, hg_out, loss_out):
    out_ref[...] = jnp.dot(ht_ref[...], grad_ref[...], preferred_element_type=F32).astype(BF16)

    @pl.when(pl.program_id(0) == 0)
    def _():
        for g in range(8):
            hg_out[:, pl.ds(g * CHUNK, CHUNK)] = hg_ref[g]
        loss_out[...] = loss_ref[0]


def per_device(hidden_states, head_weight, teacher_codes, teacher_scales, targets):
    hidden = hidden_states.reshape(2, 8, CHUNK).transpose(1, 0, 2).reshape(2, 4, 2, CHUNK)
    scales = teacher_scales.reshape(2, 4, 128).transpose(1, 0, 2)
    codes = teacher_codes.reshape(2, 128, 512).transpose(1, 0, 2).reshape(2, 2, 4, 4, 2, 2, 512)
    weight = head_weight.reshape(8, CHUNK, 512)

    vmem = pltpu.VMEM
    scratch = [
        vmem((2, 4, 4, 4, 16, WIDE), BF16),
        vmem((8, CHUNK, 512), BF16),
        vmem((2, 4, 2, WIDE), BF16),
        vmem((2, 4, 2, WIDE), BF16),
        vmem((4, 2, 2, 4, 2, 2, 512), BF16),
        vmem((4, 4, 2, 4, 2, 512), BF16),
        vmem((4, 4, 4, 2, 2, 512), BF16),
        vmem((2, 4, 4, 4, 2, 512), BF16),
        vmem((256, 512), F32),
        vmem((256, 512), F32),
        vmem((256, 512), BF16),
        vmem((8, CHUNK, 256), BF16),
        vmem((8, 8, 256), F32),
        vmem((16, 8, 256), F32),
        vmem((4, 4, 4, 16, CHUNK), F32),
        vmem((4, 4, 4, 16, CHUNK), BF16),
        vmem((4, 4, 4, 16, CHUNK), BF16),
        vmem((4, 4, 4, 16, CHUNK), BF16),
    ]
    widths = [part[2] for part in PARTS]
    forwarded = [(4, 2, 16, widths[0]), (2, 2, 2, 16, widths[1]), (2, 2, 2, 16, widths[2])]
    arrived = [(4, 4, 16, widths[0]), (2, 2, 4, 16, widths[1]), (2, 2, 4, 16, widths[2])]
    scratch += [vmem(shape, BF16) for shape in forwarded * 2 + arrived * 2]
    scratch += [vmem((4, 4, 16, n), F32) for n in widths]
    scratch += [vmem((4, 4, 16, n), BF16) for n in widths]
    scratch += [vmem((3, 4, 16, n), BF16) for n in widths]
    scratch += [vmem((4, 16, n), F32) for n in widths]
    scratch += [vmem((3, 16, n), F32) for n in widths]
    scratch += [vmem((2, 4, 2, CHUNK), F32), vmem((2, 4, 2, CHUNK), F32), vmem((8, 256), F32)]
    scratch += [
        pltpu.SemaphoreType.DMA((176,)),
        pltpu.SemaphoreType.DMA((176,)),
        pltpu.SemaphoreType.DMA((16,)),
    ]
    hidden_grad, loss, grad, hidden_t = pl.pallas_call(
        kernel,
        out_shape=(
            jax.ShapeDtypeStruct((2, 4, 2, CHUNK), F32),
            jax.ShapeDtypeStruct((8, 256), F32),
            jax.ShapeDtypeStruct((256, 512), BF16),
            jax.ShapeDtypeStruct((8, CHUNK, 256), BF16),
        ),
        in_specs=[pl.BlockSpec(memory_space=pl.ANY)] * 4 + [pl.BlockSpec(memory_space=pltpu.VMEM)],
        out_specs=[pl.BlockSpec(memory_space=pl.ANY)] * 4,
        scratch_shapes=scratch,
        compiler_params=pltpu.CompilerParams(
            collective_id=0, has_side_effects=True, vmem_limit_bytes=60 * 1024 * 1024
        ),
    )(hidden, weight, codes, scales, targets.reshape(1, 256))

    head_grad, hidden_grad, token_loss = pl.pallas_call(
        head_kernel,
        grid=(8,),
        out_shape=(
            jax.ShapeDtypeStruct((8192, 512), BF16),
            jax.ShapeDtypeStruct((2, 8192), F32),
            jax.ShapeDtypeStruct((256,), F32),
        ),
        in_specs=[
            pl.BlockSpec((CHUNK, 256), lambda g: (g, 0)),
            pl.BlockSpec((256, 512), lambda g: (0, 0)),
            pl.BlockSpec((8, 2, CHUNK), lambda g: (0, 0, 0)),
            pl.BlockSpec((8, 256), lambda g: (0, 0)),
        ],
        out_specs=(
            pl.BlockSpec((CHUNK, 512), lambda g: (g, 0)),
            pl.BlockSpec((2, 8192), lambda g: (0, 0)),
            pl.BlockSpec((256,), lambda g: (0,)),
        ),
        compiler_params=pltpu.CompilerParams(vmem_limit_bytes=60 * 1024 * 1024),
    )(hidden_t.reshape(8192, 256), grad, hidden_grad.reshape(8, 2, CHUNK), loss)
    return hidden_grad, head_grad, token_loss


def solution(mesh):
    return jax.shard_map(
        per_device,
        mesh=mesh,
        in_specs=(
            P(AXES, None),
            P(None, AXES),
            P(AXES, None),
            P(AXES, None),
            P(),
        ),
        out_specs=(P(AXES, None), P(None, AXES), P()),
        check_vma=False,
    )
```

time: 93.3 us -> 86.1 us (0.923)
  local copies, waits for them, and re-layouts: 7.11 us -> 0 us
    unnamed x7 -> x0, local copies, waits for them, and re-layouts: 3.77 us -> none
    reshape x3 -> x0, local copies, waits for them, and re-layouts: 2.34 us -> none  [the longest x2 1.63 us: per_device(): targets.reshape(2, 2, 4, 4, 2, 2).transpose(2, 0, 4, 3, 1, 5)]
where the time goes in v2:
time: 86.1 us; the launch traced here: 85.8 us
  Pallas kernels  85.1 us (99%)
    pallas_call x1, Pallas kernels, per_device(): pl.pallas_call(kernel, out_shape=(jax.ShapeDtypeStruct((2, 4, 2, CHUNK),...  76.3 us
    pallas_call x1, Pallas kernels, per_device(): pl.pallas_call(head_kernel, grid=(8,), out_shape=(jax.ShapeDtypeStruct((8...  8.86 us

profile of v2, /device:TPU:1, one launch (start us, length us, event | category | flops | bytes accessed | tf_op | source)
XLA Modules:
  0.0 85.8 jit_solution(10594490884636002258)
XLA Ops:
  0.6 76.3 %shard_map.76 = (f32[2,4,2,1024]{3,2,1,0:T(2,128)}, f32[8,256]{1,0:T(8,128)}, bf16[256,512]{1,0:T(8,128)(2,1)}, bf16[8,1024,256]{2,1,0:T(8,128)(2,1)}) custom-call(bf16[2,4,2,1024]{3,2,1,0:T(2,128)(2,1)} %bitcast.21, bf16[8,1024,512]{2,1,0:T(8,128)(2,1)} %bitcast.17, bf16[2,2,4,4,2,2,512]{6,5,4,3,2,1,0:T(2,128)(2,1)} %bitcast.19, ...), custom_call_target="tpu_custom_call" | custom-call | tf_op jit(solution)/shard_map/pallas_call | solution.py:491
  76.9 8.9 %shard_map.77 = (bf16[8192,512]{1,0:T(8,128)(2,1)}, f32[2,8192]{1,0:T(2,128)}, f32[256]{0:T(256)}) custom-call(bf16[8192,256]{1,0:T(8,128)(2,1)} %bitcast.18, bf16[256,512]{1,0:T(8,128)(2,1)} %get-tuple-element.11.grad_ref, f32[8,2,1024]{2,1,0:T(2,128)} %bitcast.20, f32[8,256]{1,0:T(8,128)} %get-tuple-element.13.loss_ref), custom_call_target="tpu_custom_call" | custom-call | tf_op jit(solution)/shard_map/pallas_call | solution.py:507

commit v3 on v2

--- a/solution.py
+++ b/solution.py
@@ -28,11 +28,11 @@
 def kernel(
     h_in, w_in, codes_in, scales_in, tgt_in,
     hg_out, loss_out, grad_out, ht_out,
-    h_all, w_all, src8, pre8, t1, t2, t3, t4, logits, teacher, grad_v, ht_v,
+    h_all, w_all, src8, pre8, t1, t2, t3, t4, logits, teacher,
     st_a, st_b, own, send_c, recv_c, summed,
     fl_a, fl_b, fl_c, fr_a, fr_b, fr_c, rl_a, rl_b, rl_c, rr_a, rr_b, rr_c,
     f2a, f2b, f2c, b2a, b2b, b2c, r2a, r2b, r2c,
-    f1a, f1b, f1c, r1a, r1b, r1c, fin_s, fin_r, loss_v,
+    f1a, f1b, f1c, r1a, r1b, r1c, fin_s, fin_r,
     send_sems, recv_sems, local_sems,
 ):
     dp, vo = lax.axis_index("dp"), lax.axis_index("vocab")
@@ -46,7 +46,7 @@
         return lax.rem(me[axis] + k, 2 if axis == "c" else 4)
 
     count = {"remote": 0, "local": 0}
-    unsent, unstored = [], []
+    unsent = []
 
     def push(src, dst, **other):
         n = count["remote"]
@@ -77,15 +77,6 @@
     heads += [local(scales_in, src8.at[c, :, :, pl.ds(CHUNK, 128)]) for c in range(2)]
     own_codes = local(codes_in.at[:, :, me["x"]], t1.at[me["x"]])
     w_copy = local(w_in, w_all)
-    for copy in heads:
-        copy.wait()
-    pl.semaphore_wait(barrier, len(partners))
-
-    arriving = []
-    for k, e in group:
-        z, c = step("z", k), step("c", e)
-        arriving.append(push(src8.at[c, z], pre8.at[me["c"], me["z"]], z=z, c=c))
-    pre8[me["c"], me["z"]] = src8[me["c"], me["z"]]
     k_row = lax.broadcasted_iota(jnp.int32, (256, 256), 0)
     n_col = lax.broadcasted_iota(jnp.int32, (256, 256), 1)
     natural = (
@@ -96,6 +87,16 @@
     target = jnp.sum(jnp.where(reorder, tgt_in[...].astype(F32), 0.0), axis=1, keepdims=True)
     first = (dp * 32 + vo) * 512
     hit = (first + lax.broadcasted_iota(jnp.int32, (256, 512), 1)).astype(F32) == target
+    for copy in heads:
+        copy.wait()
+    pl.semaphore_wait(barrier, len(partners))
+
+    arriving = []
+    for k, e in group:
+        z, c = step("z", k), step("c", e)
+        arriving.append(push(src8.at[c, z], pre8.at[me["c"], me["z"]], z=z, c=c))
+    pre8[me["c"], me["z"]] = src8[me["c"], me["z"]]
+    codes_wave = [push(codes_in.at[:, :, step("x", k)], t1.at[me["x"]], x=step("x", k)) for k in (2, 1, 3)]
     for copy in arriving:
         copy.wait_recv()
     h_all[me["c"], me["z"], me["x"], me["y"]] = jnp.concatenate(
@@ -122,11 +123,6 @@
         return [push(view, view, **{axis: step(axis, k)}) for k in (2, 1, 3)]
 
     wave = [gather_phase(part, 0) for part in PARTS]
-    codes_wave = [push(codes_in.at[:, :, step("x", k)], t1.at[me["x"]], x=step("x", k)) for k in (2, 1, 3)]
-    for i, part in enumerate(PARTS):
-        for copy in wave[i]:
-            copy.wait_recv()
-        wave[i] = gather_phase(part, 1)
     for copy in codes_wave:
         copy.wait_recv()
     own_codes.wait()
@@ -135,6 +131,14 @@
         for k in (2, 1, 3)
     ]
     t2[me["y"]] = t1[:, me["y"] // 2, :, :, me["y"] % 2]
+    for i, part in enumerate(PARTS):
+        for copy in wave[i]:
+            copy.wait_recv()
+        wave[i] = gather_phase(part, 1)
+    for copy in codes_wave:
+        copy.wait_recv()
+    codes_wave = [push(t2.at[:, :, :, step("z", k)], t3.at[me["z"]], z=step("z", k)) for k in (2, 1, 3)]
+    t3[me["z"]] = t2[:, :, :, me["z"]]
 
     other_core = step("c", 1)
     crossing, right, left = [], [], []
@@ -165,8 +169,8 @@
         forward.append((up, ring(part, step(part[3][2], 1), 1, 3)))
     for copy in codes_wave:
         copy.wait_recv()
-    codes_wave = [push(t2.at[:, :, :, step("z", k)], t3.at[me["z"]], z=step("z", k)) for k in (2, 1, 3)]
-    t3[me["z"]] = t2[:, :, :, me["z"]]
+    codes_core = push(t3.at[:, :, :, other_core], t4.at[me["c"]], c=other_core)
+    t4[me["c"]] = t3[:, :, :, me["c"]]
     for i, part in enumerate(PARTS):
         right[i][1].wait_recv()
         cross(part, step(part[3][2], 3))
@@ -177,10 +181,6 @@
         cross(part, step(part[3][2], 2), 0)
         forward[i][1].wait_recv()
         cross(part, step(part[3][2], 2), 1)
-    for copy in codes_wave:
-        copy.wait_recv()
-    codes_core = push(t3.at[:, :, :, other_core], t4.at[me["c"]], c=other_core)
-    t4[me["c"]] = t3[:, :, :, me["c"]]
 
     w_copy.wait()
     logits[...] = jnp.zeros_like(logits)
@@ -241,8 +241,7 @@
     def transpose_chunks(c):
         @pl.loop(0, 4)
         def _(z):
-            ht_v[c * 4 + z] = h_all[c, z, :, :, :, pl.ds(0, CHUNK)].reshape(256, CHUNK).T
-        unstored.append(local(ht_v.at[pl.ds(c * 4, 4)], ht_out.at[pl.ds(c * 4, 4)]))
+            ht_out[c * 4 + z] = h_all[c, z, :, :, :, pl.ds(0, CHUNK)].reshape(256, CHUNK).T
 
     st_a[0] = mine
     copies = [
@@ -271,12 +270,11 @@
         - jnp.exp(teacher[...] - columns[:, 1:2])
         - CE_WEIGHT * hit.astype(F32)
     )
-    grad_v[...] = grad.astype(BF16)
-    unstored.append(local(grad_v, grad_out))
+    grad_out[...] = grad.astype(BF16)
 
     def partial_of(c, j):
         return lax.dot_general(
-            grad_v[...], w_all[c * 4 + step("z", Z_ORDER[j])], (((1,), (1,)), ((), ())), preferred_element_type=F32
+            grad_out[...], w_all[c * 4 + step("z", Z_ORDER[j])], (((1,), (1,)), ((), ())), preferred_element_type=F32
         ).reshape(4, 4, 16, CHUNK)
 
     crossing = []
@@ -407,10 +405,9 @@
             )
             for k in (2, 1, 3)
         ]
-    loss_v[...] = jnp.broadcast_to(
+    loss_out[...] = jnp.broadcast_to(
         jnp.sum(jnp.where(reorder, columns[:, 2:3], 0.0), axis=0, keepdims=True), (8, 256)
     )
-    unstored.append(local(loss_v, loss_out))
     for i, part in enumerate(PARTS):
         for copy in waves[i]:
             copy.wait_recv()
@@ -429,21 +426,23 @@
     fin_r[me["c"], me["z"]] = fin_s[me["c"], me["z"]]
     for copy in arriving:
         copy.wait_recv()
-    unstored.append(local(fin_r, hg_out))
+    hg_out[...] = fin_r[...]
     for copy in unsent:
         copy.wait_send()
-    for copy in unstored:
+
+
+def head_kernel(ht_ref, grad_ref, hg_ref, loss_ref, out_ref, hg_out, loss_out, out_v, sems):
+    copies = []
+    for g in range(8):
+        out_v[g] = jnp.dot(ht_ref[g], grad_ref[...], preferred_element_type=F32).astype(BF16)
+        copy = pltpu.make_async_copy(out_v.at[g], out_ref.at[pl.ds(g * CHUNK, CHUNK)], sems.at[g])
+        copy.start()
+        copies.append(copy)
+    for g in range(8):
+        hg_out[:, pl.ds(g * CHUNK, CHUNK)] = hg_ref[g]
+    loss_out[...] = loss_ref[0]
+    for copy in copies:
         copy.wait()
-
-
-def head_kernel(ht_ref, grad_ref, hg_ref, loss_ref, out_ref, hg_out, loss_out):
-    out_ref[...] = jnp.dot(ht_ref[...], grad_ref[...], preferred_element_type=F32).astype(BF16)
-
-    @pl.when(pl.program_id(0) == 0)
-    def _():
-        for g in range(8):
-            hg_out[:, pl.ds(g * CHUNK, CHUNK)] = hg_ref[g]
-        loss_out[...] = loss_ref[0]
 
 
 def per_device(hidden_states, head_weight, teacher_codes, teacher_scales, targets):
@@ -464,8 +463,6 @@
         vmem((2, 4, 4, 4, 2, 512), BF16),
         vmem((256, 512), F32),
         vmem((256, 512), F32),
-        vmem((256, 512), BF16),
-        vmem((8, CHUNK, 256), BF16),
         vmem((8, 8, 256), F32),
         vmem((16, 8, 256), F32),
         vmem((4, 4, 4, 16, CHUNK), F32),
@@ -482,7 +479,7 @@
     scratch += [vmem((3, 4, 16, n), BF16) for n in widths]
     scratch += [vmem((4, 16, n), F32) for n in widths]
     scratch += [vmem((3, 16, n), F32) for n in widths]
-    scratch += [vmem((2, 4, 2, CHUNK), F32), vmem((2, 4, 2, CHUNK), F32), vmem((8, 256), F32)]
+    scratch += [vmem((2, 4, 2, CHUNK), F32), vmem((2, 4, 2, CHUNK), F32)]
     scratch += [
         pltpu.SemaphoreType.DMA((176,)),
         pltpu.SemaphoreType.DMA((176,)),
@@ -491,40 +488,31 @@
     hidden_grad, loss, grad, hidden_t = pl.pallas_call(
         kernel,
         out_shape=(
-            jax.ShapeDtypeStruct((2, 4, 2, CHUNK), F32),
-            jax.ShapeDtypeStruct((8, 256), F32),
-            jax.ShapeDtypeStruct((256, 512), BF16),
-            jax.ShapeDtypeStruct((8, CHUNK, 256), BF16),
+            pltpu.VMEM((2, 4, 2, CHUNK), F32),
+            pltpu.VMEM((8, 256), F32),
+            pltpu.VMEM((256, 512), BF16),
+            pltpu.VMEM((8, CHUNK, 256), BF16),
         ),
-        in_specs=[pl.BlockSpec(memory_space=pl.ANY)] * 4 + [pl.BlockSpec(memory_space=pltpu.VMEM)],
-        out_specs=[pl.BlockSpec(memory_space=pl.ANY)] * 4,
+        in_specs=[pl.BlockSpec(memory_space=pltpu.HBM)] * 4 + [pl.BlockSpec(memory_space=pltpu.VMEM)],
+        out_specs=[pl.BlockSpec(memory_space=pltpu.VMEM)] * 4,
         scratch_shapes=scratch,
         compiler_params=pltpu.CompilerParams(
-            collective_id=0, has_side_effects=True, vmem_limit_bytes=60 * 1024 * 1024
+            collective_id=0, has_side_effects=True, vmem_limit_bytes=61500000
         ),
     )(hidden, weight, codes, scales, targets.reshape(1, 256))
 
     head_grad, hidden_grad, token_loss = pl.pallas_call(
         head_kernel,
-        grid=(8,),
         out_shape=(
             jax.ShapeDtypeStruct((8192, 512), BF16),
             jax.ShapeDtypeStruct((2, 8192), F32),
             jax.ShapeDtypeStruct((256,), F32),
         ),
-        in_specs=[
-            pl.BlockSpec((CHUNK, 256), lambda g: (g, 0)),
-            pl.BlockSpec((256, 512), lambda g: (0, 0)),
-            pl.BlockSpec((8, 2, CHUNK), lambda g: (0, 0, 0)),
-            pl.BlockSpec((8, 256), lambda g: (0, 0)),
-        ],
-        out_specs=(
-            pl.BlockSpec((CHUNK, 512), lambda g: (g, 0)),
-            pl.BlockSpec((2, 8192), lambda g: (0, 0)),
-            pl.BlockSpec((256,), lambda g: (0,)),
-        ),
-        compiler_params=pltpu.CompilerParams(vmem_limit_bytes=60 * 1024 * 1024),
-    )(hidden_t.reshape(8192, 256), grad, hidden_grad.reshape(8, 2, CHUNK), loss)
+        in_specs=[pl.BlockSpec(memory_space=pltpu.VMEM)] * 4,
+        out_specs=[pl.BlockSpec(memory_space=pltpu.HBM)] + [pl.BlockSpec(memory_space=pltpu.VMEM)] * 2,
+        scratch_shapes=[pltpu.VMEM((8, CHUNK, 512), BF16), pltpu.SemaphoreType.DMA((8,))],
+        compiler_params=pltpu.CompilerParams(vmem_limit_bytes=40 * 1024 * 1024),
+    )(hidden_t, grad, hidden_grad.reshape(8, 2, CHUNK), loss)
     return hidden_grad, head_grad, token_loss
 
 

time: 86.1 us -> 81 us (0.941)
  Pallas kernels: 85.1 us -> 80.3 us
    pallas_call x2, Pallas kernels: 85.1 us -> 80.3 us  [the longest x1 75.8 us: per_device(): pl.pallas_call(kernel, out_shape=(pltpu.VMEM((2, 4, 2, CHUNK), F32), pltp...]
where the time goes in v3:
time: 81 us; the launch traced here: 80.9 us
  Pallas kernels  80.3 us (99%)
    pallas_call x1, Pallas kernels, per_device(): pl.pallas_call(kernel, out_shape=(pltpu.VMEM((2, 4, 2, CHUNK), F32), pltp...  75.8 us
    pallas_call x1, Pallas kernels, per_device(): pl.pallas_call(head_kernel, out_shape=(jax.ShapeDtypeStruct((8192, 512),...  4.43 us

profile of v3, /device:TPU:1, one launch (start us, length us, event | category | flops | bytes accessed | tf_op | source)
XLA Modules:
  0.0 80.9 jit_solution(1133426029586043382)
XLA Ops:
  0.6 75.8 %shard_map.76 = (f32[2,4,2,1024]{3,2,1,0:T(2,128)S(1)}, f32[8,256]{1,0:T(8,128)S(1)}, bf16[256,512]{1,0:T(8,128)(2,1)S(1)}, bf16[8,1024,256]{2,1,0:T(8,128)(2,1)S(1)}) custom-call(bf16[2,4,2,1024]{3,2,1,0:T(2,128)(2,1)} %bitcast.19, bf16[8,1024,512]{2,1,0:T(8,128)(2,1)} %bitcast.17, bf16[2,2,4,4,2,2,512]{6,5,4,3,2,1,0:T(2,128)(2,1)} %bitcast.18, ...), custom_call_target="tpu_custom_call" | custom-call | tf_op jit(solution)/shard_map/pallas_call | solution.py:488
  76.5 4.4 %shard_map.77 = (bf16[8192,512]{1,0:T(8,128)(2,1)}, f32[2,8192]{1,0:T(2,128)}, f32[256]{0:T(256)}) custom-call(bf16[8,1024,256]{2,1,0:T(8,128)(2,1)S(1)} %get-tuple-element.10.ht_ref, bf16[256,512]{1,0:T(8,128)(2,1)S(1)} %get-tuple-element.11.grad_ref, f32[8,2,1024]{2,1,0:T(2,128)S(1)} %bitcast.16, f32[8,256]{1,0:T(8,128)S(1)} %get-tuple-element.13.loss_ref), custom_call_target="tpu_custom_call" | custom-call | tf_op jit(solution)/shard_map/pallas_call | solution.py:504

commit v4 on v3

v4 whole, which is shorter than its diff:
```python
import functools

import jax
import jax.numpy as jnp
from jax import lax
from jax.experimental import pallas as pl
from jax.experimental.pallas import tpu as pltpu
from jax.sharding import PartitionSpec as P

GRAD_SCALE = 32.0
CE_WEIGHT = 0.5
F32, BF16 = jnp.float32, jnp.bfloat16
MESH = pl.DeviceIdType.MESH
AXES = ("dp", "vocab")

CHUNK = 1024
HALF = 4096
BLOCK_A, WIDE = 384, 1536
HIDDEN_C = HALF - 2 * WIDE
Z_ORDER = (2, 1, 3, 0)


def kernel(
    h_in, w_in, codes_in, scales_in, tgt_in,
    hg_out, loss_out, grad_out, ht_out,
    w_all, src, pre, send_a, recv_a, rows_b, rows_c, h_a, h_b, h_c,
    t1, t2, t3, t4, logits, teacher, st_a, st_b,
    own_a, own_b, own_c, to_a, to_b, to_c, from_a, from_b, from_c, sum_a, sum_b, sum_c,
    fl_a, fl_b, fl_c, fr_a, fr_b, fr_c, rl_a, rl_b, rl_c, rr_a, rr_b, rr_c,
    acc_a, acc_b, acc_c, out_a, out_b, out_c, in_a, in_b, in_c, keep_b,
    rest_a, rest_b, rest_c, last_a, last_b, last_c, fin_s, fin_r,
    send_sems, recv_sems, local_sems,
):
    dp, vo = lax.axis_index("dp"), lax.axis_index("vocab")
    me = {"x": vo // 8, "z": (vo // 2) % 4, "y": (dp // 2) * 2 + vo % 2, "c": dp % 2}

    def device(**other):
        at = {**me, **other}
        return ((at["y"] // 2) * 2 + at["c"], (at["x"] * 4 + at["z"]) * 2 + at["y"] % 2)

    def step(axis, k):
        return lax.rem(me[axis] + k, 2 if axis == "c" else 4)

    count = {"remote": 0, "local": 0}
    unsent = []

    def push(src, dst, **other):
        n = count["remote"]
        count["remote"] += 1
        copy = pltpu.make_async_remote_copy(
            src_ref=src, dst_ref=dst, send_sem=send_sems.at[n], recv_sem=recv_sems.at[n],
            device_id=device(**other), device_id_type=MESH,
        )
        copy.start()
        unsent.append(copy)
        return copy

    def local(src, dst):
        n = count["local"]
        count["local"] += 1
        copy = pltpu.make_async_copy(src, dst, local_sems.at[n])
        copy.start()
        return copy

    barrier = pltpu.get_barrier_semaphore()
    partners = [dict(x=step("x", i), y=step("y", k)) for i in range(4) for k in range(4) if (i, k) != (0, 0)]
    group = [(k, e) for k in range(4) for e in range(2) if (k, e) != (0, 0)]
    partners += [dict(z=step("z", k), c=step("c", e)) for k, e in group]
    for other in partners:
        pl.semaphore_signal(barrier, inc=1, device_id=device(**other), device_id_type=MESH)

    heads = [local(h_in.at[:, pl.ds(c * HALF, HALF)], src.at[c, :, pl.ds(0, HALF)]) for c in range(2)]
    heads += [local(scales_in, src.at[c, :, pl.ds(HALF, 512)]) for c in range(2)]
    own_codes = local(codes_in.at[:, :, me["x"]], t1.at[me["x"]])
    w_copy = local(w_in, w_all)
    k_row = lax.broadcasted_iota(jnp.int32, (256, 256), 0)
    n_col = lax.broadcasted_iota(jnp.int32, (256, 256), 1)
    natural = (
        ((k_row >> 5) & 1) * 128 + ((k_row >> 1) & 1) * 64 + (k_row >> 6) * 16
        + ((k_row >> 2) & 3) * 4 + ((k_row >> 4) & 1) * 2 + (k_row & 1)
    )
    reorder = natural == n_col
    target = jnp.sum(jnp.where(reorder, tgt_in[...].astype(F32), 0.0), axis=1, keepdims=True)
    first = (dp * 32 + vo) * 512
    hit = (first + lax.broadcasted_iota(jnp.int32, (256, 512), 1)).astype(F32) == target
    for copy in heads:
        copy.wait()
    pl.semaphore_wait(barrier, len(partners))

    other_core = step("c", 1)
    swap = push(src.at[other_core], pre.at[me["c"]], c=other_core)
    codes_wave = [push(codes_in.at[:, :, step("x", k)], t1.at[me["x"]], x=step("x", k)) for k in (2, 1, 3)]
    pre[me["c"]] = src[me["c"]]
    swap.wait_recv()
    rows = jnp.concatenate([pre[0].astype(F32), pre[1].astype(F32)], axis=0).astype(BF16)
    for z in range(4):
        send_a[z] = rows[:, z * BLOCK_A : (z + 1) * BLOCK_A]
    rows_b[me["y"], me["z"]] = rows[:, WIDE : 2 * WIDE]
    rows_c[me["x"], me["z"]] = rows[:, 2 * WIDE :]

    def spread(src_ref, dst_ref, axis):
        return [push(src_ref, dst_ref, **{axis: step(axis, k)}) for k in (2, 1, 3)]

    def pack(pieces):
        return jnp.concatenate([p.astype(F32) for p in pieces], axis=0).astype(BF16)

    wave_b = spread(rows_b.at[me["y"], me["z"]], rows_b.at[me["y"], me["z"]], "y")
    wave_c = spread(rows_c.at[me["x"], me["z"]], rows_c.at[me["x"], me["z"]], "z")
    wave_a = [push(send_a.at[step("z", k)], recv_a.at[me["z"]], z=step("z", k)) for k in (2, 1, 3)]
    recv_a[me["z"]] = send_a[me["z"]]
    own_codes.wait()

    for copy in wave_b:
        copy.wait_recv()
    wave_b = spread(rows_b.at[:, me["z"]], rows_b.at[:, me["z"]], "z")
    for copy in wave_c:
        copy.wait_recv()
    h_c[me["c"], me["x"], me["y"]] = pack([rows_c[me["x"], z] for z in range(4)])
    view = h_c.at[me["c"], me["x"], me["y"]]
    wave_c = spread(view, view, "x")
    for copy in wave_a:
        copy.wait_recv()
    h_a[me["c"], me["z"], me["x"], me["y"]] = pack([recv_a[z] for z in range(4)])
    view = h_a.at[me["c"], me["z"], me["x"], me["y"]]
    plane = [(i, k) for i in range(4) for k in range(4) if (i, k) != (0, 0)]
    wave_a = [push(view, view, x=step("x", i), y=step("y", k)) for i, k in plane]
    for copy in codes_wave:
        copy.wait_recv()
    codes_wave = [
        push(t1.at[:, step("y", k) // 2, :, :, step("y", k) % 2], t2.at[me["y"]], y=step("y", k))
        for k in (2, 1, 3)
    ]
    t2[me["y"]] = t1[:, me["y"] // 2, :, :, me["y"] % 2]

    full, half0, half1 = slice(None), pl.ds(0, 2), pl.ds(2, 2)
    ring_axis = ("z", "x", "y")

    def block(i, coordinate, half):
        if i == 0:
            return h_a.at[me["c"], coordinate, half]
        if i == 1:
            return h_b.at[me["c"], coordinate, half]
        return h_c.at[me["c"], half, coordinate]

    def ring(i, coordinate, half, k):
        view, axis = block(i, coordinate, half), ring_axis[i]
        return push(view, view, **{axis: step(axis, k)})

    crossing, right, left = [], [None] * 3, [None] * 3

    def cross(i, coordinate, half=full):
        view = block(i, coordinate, half)
        crossing.append(push(view, view, c=other_core))

    def start_ring(i):
        here = me[ring_axis[i]]
        up0, down1 = ring(i, here, half0, 1), ring(i, here, half1, 3)
        right[i] = [up0, ring(i, here, half1, 1)]
        left[i] = [ring(i, here, half0, 3), down1]

    for copy in wave_c:
        copy.wait_recv()
    start_ring(2)
    for copy in wave_b:
        copy.wait_recv()
    for y in range(4):
        h_b[me["c"], me["x"], y] = pack([rows_b[y, z] for z in range(4)])
    start_ring(1)
    for copy in wave_a:
        copy.wait_recv()
    start_ring(0)
    for i in (2, 1, 0):
        cross(i, me[ring_axis[i]])
    for copy in codes_wave:
        copy.wait_recv()
    codes_wave = [push(t2.at[:, :, :, step("z", k)], t3.at[me["z"]], z=step("z", k)) for k in (2, 1, 3)]
    t3[me["z"]] = t2[:, :, :, me["z"]]
    forward = [None] * 3
    for i in (2, 1, 0):
        right[i][0].wait_recv()
        up = ring(i, step(ring_axis[i], 3), half0, 1)
        left[i][1].wait_recv()
        forward[i] = (up, ring(i, step(ring_axis[i], 1), half1, 3))
    for i in (2, 1, 0):
        right[i][1].wait_recv()
        cross(i, step(ring_axis[i], 3))
        left[i][0].wait_recv()
        cross(i, step(ring_axis[i], 1))
    for copy in codes_wave:
        copy.wait_recv()
    codes_core = push(t3.at[:, :, :, other_core], t4.at[me["c"]], c=other_core)
    t4[me["c"]] = t3[:, :, :, me["c"]]
    for i in (2, 1, 0):
        forward[i][0].wait_recv()
        cross(i, step(ring_axis[i], 2), half0)
        forward[i][1].wait_recv()
        cross(i, step(ring_axis[i], 2), half1)

    w_copy.wait()
    logits[...] = jnp.zeros_like(logits)

    def add_logits(c):
        for ref, first, width in ((h_b, WIDE, WIDE), (h_c, 2 * WIDE, HIDDEN_C)):
            rows = ref[c, :, :, :, pl.ds(0, width)].reshape(256, width)
            logits[...] += jnp.dot(rows, w_all[c, pl.ds(first, width), :], preferred_element_type=F32)
        rows = jnp.concatenate([h_a[c, z].reshape(256, BLOCK_A) for z in range(4)], axis=1)
        logits[...] += jnp.dot(rows, w_all[c, pl.ds(0, WIDE), :], preferred_element_type=F32)

    add_logits(me["c"])
    block_row = lax.broadcasted_iota(jnp.int32, (512, 512), 0)
    column = lax.broadcasted_iota(jnp.int32, (512, 512), 1)
    pick = (block_row == dp * 128 + vo * 4 + column // 128).astype(F32).astype(BF16)
    scale = jnp.dot(
        h_c[me["c"], :, :, :, pl.ds(HIDDEN_C, 512)].reshape(256, 512), pick, preferred_element_type=F32
    )
    codes_core.wait_recv()
    for x in range(4):
        for y in range(4):
            row = (x * 4 + y) * 16
            code = jnp.concatenate(
                [t4[c, z, y, x].astype(F32) for z in range(4) for c in range(2)], axis=0
            )
            teacher[pl.ds(row, 16), :] = code * scale[row : row + 16]
    for copy in crossing:
        copy.wait_recv()
    add_logits(other_core)

    lg, tc = logits[...], teacher[...]
    m_s = jnp.max(lg, axis=1, keepdims=True)
    m_t = jnp.max(tc, axis=1, keepdims=True)
    w_t = jnp.exp(tc - m_t)
    stats = (
        m_s, jnp.sum(jnp.exp(lg - m_s), axis=1, keepdims=True),
        m_t, jnp.sum(w_t, axis=1, keepdims=True),
        jnp.sum(w_t * (tc - lg), axis=1, keepdims=True),
        jnp.sum(jnp.where(hit, lg, 0.0), axis=1, keepdims=True),
    )
    lane = lax.broadcasted_iota(jnp.int32, (256, 128), 1)
    packed = jnp.zeros((256, 128), F32)
    for n, value in enumerate(stats):
        packed = jnp.where(lane == n, value, packed)
    mine = packed.T[:8]

    def merge(parts):
        m1 = functools.reduce(jnp.maximum, [p[0:1] for p in parts])
        m2 = functools.reduce(jnp.maximum, [p[2:3] for p in parts])
        e1 = [jnp.exp(p[0:1] - m1) for p in parts]
        e2 = [jnp.exp(p[2:3] - m2) for p in parts]
        s1 = sum(p[1:2] * e for p, e in zip(parts, e1))
        s2 = sum(p[3:4] * e for p, e in zip(parts, e2))
        cross_sum = sum(p[4:5] * e for p, e in zip(parts, e2))
        target = sum(p[5:6] for p in parts)
        pad = jnp.zeros((2, 256), F32)
        return jnp.concatenate([m1, s1, m2, s2, cross_sum, target, pad], axis=0)

    def transpose_half(c):
        for z in range(4):
            ht_out[pl.ds(c * HALF + z * BLOCK_A, BLOCK_A), :] = h_a[c, z].reshape(256, BLOCK_A).T
        for ref, first, width in ((h_b, WIDE, WIDE), (h_c, 2 * WIDE, HIDDEN_C)):
            ht_out[pl.ds(c * HALF + first, width), :] = ref[c, :, :, :, pl.ds(0, width)].reshape(256, width).T

    st_a[0] = mine
    copies = [
        push(st_a.at[0], st_a.at[1 + n], z=step("z", k), c=step("c", e)) for n, (k, e) in enumerate(group)
    ]
    transpose_half(0)
    for copy in copies:
        copy.wait_recv()
    mine = merge([st_a[k] for k in range(8)])
    st_b[0] = mine
    copies = [
        push(st_b.at[0], st_b.at[1 + n], x=step("x", i), y=step("y", k)) for n, (i, k) in enumerate(plane)
    ]
    transpose_half(1)
    for copy in copies:
        copy.wait_recv()
    mine = merge([st_b[k] for k in range(16)])

    log_s = mine[0:1] + jnp.log(mine[1:2])
    log_t = mine[2:3] + jnp.log(mine[3:4])
    loss = mine[4:5] / mine[3:4] - log_t + log_s + CE_WEIGHT * (log_s - mine[5:6])
    columns = jnp.concatenate([log_s, log_t, loss, jnp.zeros((125, 256), F32)], axis=0).T
    grad = GRAD_SCALE * (
        (1.0 + CE_WEIGHT) * jnp.exp(logits[...] - columns[:, 0:1])
        - jnp.exp(teacher[...] - columns[:, 1:2])
        - CE_WEIGHT * hit.astype(F32)
    )
    grad_out[...] = grad.astype(BF16)

    own, to, came = (own_a, own_b, own_c), (to_a, to_b, to_c), (from_a, from_b, from_c)
    summed = (sum_a, sum_b, sum_c)
    fl, fr, rl, rr = (fl_a, fl_b, fl_c), (fr_a, fr_b, fr_c), (rl_a, rl_b, rl_c), (rr_a, rr_b, rr_c)
    widths = (BLOCK_A, WIDE // 2, HIDDEN_C // 2)
    first_of = (0, WIDE, 2 * WIDE)
    crossing, ring_waits = {}, {}

    def partial_of(c, i, n):
        if i == 0:
            first = pl.multiple_of(step("z", Z_ORDER[n]) * BLOCK_A, 128)
        else:
            first = first_of[i] + n * widths[i]
        return lax.dot_general(
            grad_out[...], w_all[c, pl.ds(first, widths[i]), :], (((1,), (1,)), ((), ())),
            preferred_element_type=F32,
        ).reshape(4, 4, 16, widths[i])

    def pieces(i, n):
        return (2 * n, 2 * n + 1) if i == 0 else (n,)

    def send_unit(i, n):
        for p in pieces(i, n):
            to[i][p] = partial_of(other_core, i, p).astype(BF16)
        index = pl.ds(2 * n, 2) if i == 0 else n
        crossing[i, n] = push(to[i].at[index], came[i].at[index], c=other_core)

    def own_unit(i, n):
        for p in pieces(i, n):
            own[i][p] = partial_of(me["c"], i, p)

    def add_unit(i, n):
        crossing[i, n].wait_recv()
        for p in pieces(i, n):
            total = own[i][p] + came[i][p].astype(F32)
            own[i][p] = total
            summed[i][p] = total.astype(BF16)

    def block_of(i, k, n, half):
        if i == 0:
            return (Z_ORDER.index(k), half)
        if i == 1:
            return (n, step("x", k), half)
        return (n, half, step("y", k))

    def ring_push(i, k, n, half, buffer, toward):
        axis = ring_axis[i]
        place = () if i == 0 else (n,)
        if buffer is rl or buffer is rr:
            place = (*place, half)
        target = buffer[i].at[place] if place else buffer[i]
        return push(summed[i].at[block_of(i, k, n, half)], target, **{axis: step(axis, toward)})

    def ring_opposite(i, n):
        ring_waits[i, n] = [ring_push(i, 2, n, half0, fl, 1), ring_push(i, 2, n, half1, fr, 3)]

    def ring_up(i, n):
        ring_waits[i, n].append(ring_push(i, 1, n, half1, rl, 1))

    def ring_down(i, n):
        ring_waits[i, n].append(ring_push(i, 3, n, half0, rr, 3))

    def ring_forward(i, n):
        waits = ring_waits[i, n]
        for m, (k, half, ref, buffer) in enumerate(((1, half0, fl, rl), (3, half1, fr, rr))):
            waits[m].wait_recv()
            index = block_of(i, k, n, half)
            carried = ref[i][...] if i == 0 else ref[i][n]
            summed[i][index] = (own[i][index] + carried.astype(F32)).astype(BF16)
            waits.append(ring_push(i, k, n, half, buffer, k))

    def start_unit(i, n):
        ring_opposite(i, n)
        ring_up(i, n)
        ring_down(i, n)

    send_unit(0, 0)
    send_unit(1, 0)
    own_unit(0, 0)
    add_unit(0, 0)
    ring_opposite(0, 0)
    ring_up(0, 0)
    send_unit(2, 0)
    own_unit(1, 0)
    add_unit(1, 0)
    start_unit(1, 0)
    send_unit(0, 1)
    own_unit(2, 0)
    add_unit(2, 0)
    start_unit(2, 0)
    send_unit(1, 1)
    own_unit(0, 1)
    add_unit(0, 1)
    ring_down(0, 0)
    send_unit(2, 1)
    own_unit(1, 1)
    add_unit(1, 1)
    start_unit(1, 1)
    ring_forward(0, 0)
    own_unit(2, 1)
    add_unit(2, 1)
    start_unit(2, 1)
    ring_forward(1, 0)
    ring_forward(2, 0)
    ring_forward(1, 1)
    ring_forward(2, 1)

    def ring_done(i):
        for n in range(1 if i == 0 else 2):
            for copy in ring_waits[i, n][2:]:
                copy.wait_recv()

    ring_done(0)
    acc_a[...] = own_a[3] + rl_a[...].astype(F32) + rr_a[...].astype(F32)
    out_a[...] = acc_a[...].astype(BF16)
    wave_a = [
        push(out_a.at[step("x", i), step("y", k)], in_a.at[n], x=step("x", i), y=step("y", k))
        for n, (i, k) in enumerate(plane)
    ]
    ring_done(1)
    for n in range(2):
        cols = pl.ds(n * widths[1], widths[1])
        acc_b[:, :, cols] = own_b[n, me["x"]] + rl_b[n].astype(F32) + rr_b[n].astype(F32)
    for z in range(4):
        piece = acc_b[:, pl.ds(z * 4, 4), :]
        keep_b[z] = piece
        out_b[z] = piece.astype(BF16)
    wave_b = [push(out_b.at[step("z", k)], in_b.at[k - 1], z=step("z", k)) for k in (2, 1, 3)]
    ring_done(2)
    for n in range(2):
        cols = pl.ds(n * widths[2], widths[2])
        acc_c[:, :, cols] = own_c[n, :, me["y"]] + rl_c[n].astype(F32) + rr_c[n].astype(F32)
    out_c[...] = acc_c[...].astype(BF16)
    wave_c = [push(out_c.at[step("x", k)], in_c.at[k - 1], x=step("x", k)) for k in (2, 1, 3)]
    loss_out[...] = jnp.broadcast_to(
        jnp.sum(jnp.where(reorder, columns[:, 2:3], 0.0), axis=0, keepdims=True), (8, 256)
    )

    for copy in wave_b:
        copy.wait_recv()
    total = keep_b[me["z"]]
    for n in range(3):
        total = total + in_b[n].astype(F32)
    rest_b[...] = total
    wave_b = [push(rest_b.at[step("y", k)], last_b.at[k - 1], y=step("y", k)) for k in (2, 1, 3)]
    for copy in wave_c:
        copy.wait_recv()
    total = acc_c[me["x"]]
    for n in range(3):
        total = total + in_c[n].astype(F32)
    for z in range(4):
        rest_c[z] = total[z * 4 : z * 4 + 4]
    wave_c = [push(rest_c.at[step("z", k)], last_c.at[k - 1], z=step("z", k)) for k in (2, 1, 3)]
    for copy in wave_a:
        copy.wait_recv()
    total = acc_a[me["x"], me["y"]]
    for n in range(15):
        total = total + in_a[n].astype(F32)
    for z in range(4):
        rest_a[z] = total[z * 4 : z * 4 + 4]
    wave_a = [push(rest_a.at[step("z", k)], last_a.at[me["z"]], z=step("z", k)) for k in (2, 1, 3)]
    last_a[me["z"]] = rest_a[me["z"]]

    def finish(total, first, width):
        for c in range(2):
            fin_s[c, :, pl.ds(first, width)] = total[c * 2 : c * 2 + 2]

    for copy in wave_b:
        copy.wait_recv()
    finish(rest_b[me["y"]] + last_b[0] + last_b[1] + last_b[2], WIDE, WIDE)
    for copy in wave_c:
        copy.wait_recv()
    finish(rest_c[me["z"]] + last_c[0] + last_c[1] + last_c[2], 2 * WIDE, HIDDEN_C)
    for copy in wave_a:
        copy.wait_recv()
    for z in range(4):
        finish(last_a[z], z * BLOCK_A, BLOCK_A)
    swap = push(fin_s.at[other_core], fin_r, c=other_core)
    hg_out[me["c"]] = fin_s[me["c"]]
    for copy in unsent[:-1]:
        copy.wait_send()
    swap.wait_recv()
    hg_out[other_core] = fin_r[...]
    swap.wait_send()


def head_kernel(ht_ref, grad_ref, hg_ref, loss_ref, out_ref, hg_out, loss_out, out_v, sems):
    copies = []
    for g in range(8):
        out_v[g] = jnp.dot(ht_ref[pl.ds(g * CHUNK, CHUNK), :], grad_ref[...], preferred_element_type=F32).astype(BF16)
        copy = pltpu.make_async_copy(out_v.at[g], out_ref.at[pl.ds(g * CHUNK, CHUNK)], sems.at[g])
        copy.start()
        copies.append(copy)
    for c in range(2):
        hg_out[:, pl.ds(c * HALF, HALF)] = hg_ref[c]
    loss_out[...] = loss_ref[0]
    for copy in copies:
        copy.wait()


def per_device(hidden_states, head_weight, teacher_codes, teacher_scales, targets):
    codes = teacher_codes.reshape(2, 128, 512).transpose(1, 0, 2).reshape(2, 2, 4, 4, 2, 2, 512)
    weight = head_weight.reshape(2, HALF, 512)

    vmem = pltpu.VMEM
    half_b, half_c = WIDE // 2, HIDDEN_C // 2
    unit_a, unit_b, unit_c = (4, 4, 4, 16, BLOCK_A), (2, 4, 4, 16, half_b), (2, 4, 4, 16, half_c)
    forwarded = ((2, 4, 16, BLOCK_A), (2, 2, 16, half_b), (2, 2, 16, half_c))
    arrived = ((4, 4, 16, BLOCK_A), (2, 4, 16, half_b), (2, 4, 16, half_c))
    scratch = [
        vmem((2, HALF, 512), BF16),
        vmem((2, 2, HALF + 512), BF16),
        vmem((2, 2, HALF + 512), BF16),
        vmem((4, 4, BLOCK_A), BF16),
        vmem((4, 4, BLOCK_A), BF16),
        vmem((4, 4, 4, WIDE), BF16),
        vmem((4, 4, 4, WIDE), BF16),
        vmem((2, 4, 4, 4, 16, BLOCK_A), BF16),
        vmem((2, 4, 4, 16, WIDE), BF16),
        vmem((2, 4, 4, 16, WIDE), BF16),
        vmem((4, 2, 2, 4, 2, 2, 512), BF16),
        vmem((4, 4, 2, 4, 2, 512), BF16),
        vmem((4, 4, 4, 2, 2, 512), BF16),
        vmem((2, 4, 4, 4, 2, 512), BF16),
        vmem((256, 512), F32),
        vmem((256, 512), F32),
        vmem((8, 8, 256), F32),
        vmem((16, 8, 256), F32),
    ]
    scratch += [vmem(shape, F32) for shape in (unit_a, unit_b, unit_c)]
    scratch += [vmem(shape, BF16) for shape in (unit_a, unit_b, unit_c) * 3]
    scratch += [vmem(shape, BF16) for shape in forwarded * 2 + arrived * 2]
    scratch += [
        vmem((4, 4, 16, BLOCK_A), F32),
        vmem((4, 16, WIDE), F32),
        vmem((4, 16, HIDDEN_C), F32),
        vmem((4, 4, 16, BLOCK_A), BF16),
        vmem((4, 4, 4, WIDE), BF16),
        vmem((4, 16, HIDDEN_C), BF16),
        vmem((15, 16, BLOCK_A), BF16),
        vmem((3, 4, 4, WIDE), BF16),
        vmem((3, 16, HIDDEN_C), BF16),
        vmem((4, 4, 4, WIDE), F32),
        vmem((4, 4, BLOCK_A), F32),
        vmem((4, 4, WIDE), F32),
        vmem((4, 4, HIDDEN_C), F32),
        vmem((4, 4, BLOCK_A), F32),
        vmem((3, 4, WIDE), F32),
        vmem((3, 4, HIDDEN_C), F32),
        vmem((2, 2, HALF), F32),
        vmem((2, HALF), F32),
        pltpu.SemaphoreType.DMA((208,)),
        pltpu.SemaphoreType.DMA((208,)),
        pltpu.SemaphoreType.DMA((8,)),
    ]
    hidden_grad, loss, grad, hidden_t = pl.pallas_call(
        kernel,
        out_shape=(
            pltpu.VMEM((2, 2, HALF), F32),
            pltpu.VMEM((8, 256), F32),
            pltpu.VMEM((256, 512), BF16),
            pltpu.VMEM((8192, 256), BF16),
        ),
        in_specs=[pl.BlockSpec(memory_space=pltpu.HBM)] * 4 + [pl.BlockSpec(memory_space=pltpu.VMEM)],
        out_specs=[pl.BlockSpec(memory_space=pltpu.VMEM)] * 4,
        scratch_shapes=scratch,
        compiler_params=pltpu.CompilerParams(
            collective_id=0, has_side_effects=True, vmem_limit_bytes=61500000
        ),
    )(hidden_states, weight, codes, teacher_scales, targets.reshape(1, 256))

    head_grad, hidden_grad, token_loss = pl.pallas_call(
        head_kernel,
        out_shape=(
            jax.ShapeDtypeStruct((8192, 512), BF16),
            jax.ShapeDtypeStruct((2, 8192), F32),
            jax.ShapeDtypeStruct((256,), F32),
        ),
        in_specs=[pl.BlockSpec(memory_space=pltpu.VMEM)] * 4,
        out_specs=[pl.BlockSpec(memory_space=pltpu.HBM)] + [pl.BlockSpec(memory_space=pltpu.VMEM)] * 2,
        scratch_shapes=[pltpu.VMEM((8, CHUNK, 512), BF16), pltpu.SemaphoreType.DMA((8,))],
        compiler_params=pltpu.CompilerParams(vmem_limit_bytes=40 * 1024 * 1024),
    )(hidden_t, grad, hidden_grad, loss)
    return hidden_grad, head_grad, token_loss


def solution(mesh):
    return jax.shard_map(
        per_device,
        mesh=mesh,
        in_specs=(
            P(AXES, None),
            P(None, AXES),
            P(AXES, None),
            P(AXES, None),
            P(),
        ),
        out_specs=(P(AXES, None), P(None, AXES), P()),
        check_vma=False,
    )
```

time: 81 us -> 77.1 us (0.952)
  Pallas kernels: 80.3 us -> 76.3 us
    pallas_call x1, Pallas kernels: 75.8 us -> 71.9 us  [per_device(): pl.pallas_call(kernel, out_shape=(pltpu.VMEM((2, 2, HALF), F32), pltpu.VM...]
where the time goes in v4:
time: 77.1 us; the launch traced here: 77 us
  Pallas kernels  76.3 us (99%)
    pallas_call x1, Pallas kernels, per_device(): pl.pallas_call(kernel, out_shape=(pltpu.VMEM((2, 2, HALF), F32), pltpu.VM...  71.9 us
    pallas_call x1, Pallas kernels, per_device(): pl.pallas_call(head_kernel, out_shape=(jax.ShapeDtypeStruct((8192, 512),...  4.44 us

profile of v4, /device:TPU:1, one launch (start us, length us, event | category | flops | bytes accessed | tf_op | source)
XLA Modules:
  0.0 77.0 jit_solution(869700854202456111)
XLA Ops:
  0.6 71.9 %shard_map.76 = (f32[2,2,4096]{2,1,0:T(2,128)S(1)}, f32[8,256]{1,0:T(8,128)S(1)}, bf16[256,512]{1,0:T(8,128)(2,1)S(1)}, bf16[8192,256]{1,0:T(8,128)(2,1)S(1)}) custom-call(bf16[2,8192]{1,0:T(2,128)(2,1)} %h_in.1, bf16[2,4096,512]{2,1,0:T(8,128)(2,1)} %bitcast.7, bf16[2,2,4,4,2,2,512]{6,5,4,3,2,1,0:T(2,128)(2,1)} %bitcast.8, bf16[2,512]{1,0:T(2,128)(2,1)} %scales_in.1, ...), custom_call_target="tpu_custom_call" | custom-call | tf_op jit(solution)/shard_map/pallas_call | solution.py:544
  72.5 4.4 %shard_map.77 = (bf16[8192,512]{1,0:T(8,128)(2,1)}, f32[2,8192]{1,0:T(2,128)}, f32[256]{0:T(256)}) custom-call(bf16[8192,256]{1,0:T(8,128)(2,1)S(1)} %get-tuple-element.10.ht_ref, bf16[256,512]{1,0:T(8,128)(2,1)S(1)} %get-tuple-element.11.grad_ref, f32[2,2,4096]{2,1,0:T(2,128)S(1)} %get-tuple-element.12.hg_ref, f32[8,256]{1,0:T(8,128)S(1)} %get-tuple-element.13.loss_ref), custom_call_target="tpu_custom_call" | custom-call | tf_op jit(solution)/shard_map/pallas_call | solution.py:560

commit v5 on v4

--- a/solution.py
+++ b/solution.py
@@ -15,20 +15,20 @@
 
 CHUNK = 1024
 HALF = 4096
-BLOCK_A, WIDE = 384, 1536
-HIDDEN_C = HALF - 2 * WIDE
+BLOCK_A, PART_A, WIDE, HIDDEN_C = 256, 1024, 1664, 1408
+SUM_BLOCK, SUM_A, SUM_WIDE = 384, 1536, 1280
 Z_ORDER = (2, 1, 3, 0)
 
 
 def kernel(
     h_in, w_in, codes_in, scales_in, tgt_in,
-    hg_out, loss_out, grad_out, ht_out,
-    w_all, src, pre, send_a, recv_a, rows_b, rows_c, h_a, h_b, h_c,
+    hg_out, loss_out, head_out,
+    w_all, grad_v, ht, src, recv_a, rows_b, rows_c, h_a, h_b, h_c,
     t1, t2, t3, t4, logits, teacher, st_a, st_b,
     own_a, own_b, own_c, to_a, to_b, to_c, from_a, from_b, from_c, sum_a, sum_b, sum_c,
     fl_a, fl_b, fl_c, fr_a, fr_b, fr_c, rl_a, rl_b, rl_c, rr_a, rr_b, rr_c,
     acc_a, acc_b, acc_c, out_a, out_b, out_c, in_a, in_b, in_c, keep_b,
-    rest_a, rest_b, rest_c, last_a, last_b, last_c, fin_s, fin_r,
+    rest_a, rest_b, rest_c, last_a, last_b, last_c,
     send_sems, recv_sems, local_sems,
 ):
     dp, vo = lax.axis_index("dp"), lax.axis_index("vocab")
@@ -63,14 +63,14 @@
         return copy
 
     barrier = pltpu.get_barrier_semaphore()
-    partners = [dict(x=step("x", i), y=step("y", k)) for i in range(4) for k in range(4) if (i, k) != (0, 0)]
+    partners = [{axis: step(axis, k)} for axis in "xyz" for k in (2, 1, 3)]
+    partners += [{axis: step(axis, k), "c": step("c", 1)} for axis in "yz" for k in (2, 1, 3)] + [dict(c=step("c", 1))]
     group = [(k, e) for k in range(4) for e in range(2) if (k, e) != (0, 0)]
-    partners += [dict(z=step("z", k), c=step("c", e)) for k, e in group]
     for other in partners:
         pl.semaphore_signal(barrier, inc=1, device_id=device(**other), device_id_type=MESH)
 
     heads = [local(h_in.at[:, pl.ds(c * HALF, HALF)], src.at[c, :, pl.ds(0, HALF)]) for c in range(2)]
-    heads += [local(scales_in, src.at[c, :, pl.ds(HALF, 512)]) for c in range(2)]
+    heads += [local(scales_in.at[:, pl.ds(c * 256, 256)], src.at[c, :, pl.ds(HALF, 256)]) for c in range(2)]
     own_codes = local(codes_in.at[:, :, me["x"]], t1.at[me["x"]])
     w_copy = local(w_in, w_all)
     k_row = lax.broadcasted_iota(jnp.int32, (256, 256), 0)
@@ -88,26 +88,26 @@
     pl.semaphore_wait(barrier, len(partners))
 
     other_core = step("c", 1)
-    swap = push(src.at[other_core], pre.at[me["c"]], c=other_core)
-    codes_wave = [push(codes_in.at[:, :, step("x", k)], t1.at[me["x"]], x=step("x", k)) for k in (2, 1, 3)]
-    pre[me["c"]] = src[me["c"]]
-    swap.wait_recv()
-    rows = jnp.concatenate([pre[0].astype(F32), pre[1].astype(F32)], axis=0).astype(BF16)
-    for z in range(4):
-        send_a[z] = rows[:, z * BLOCK_A : (z + 1) * BLOCK_A]
-    rows_b[me["y"], me["z"]] = rows[:, WIDE : 2 * WIDE]
-    rows_c[me["x"], me["z"]] = rows[:, 2 * WIDE :]
 
     def spread(src_ref, dst_ref, axis):
         return [push(src_ref, dst_ref, **{axis: step(axis, k)}) for k in (2, 1, 3)]
 
+    wave_a, wave_b, wave_c = [], [], []
+    cols_b, cols_c = pl.ds(PART_A, WIDE), pl.ds(PART_A + WIDE, WIDE)
+    for k, e in group:
+        y, z, c = step("y", k), step("z", k), step("c", e)
+        wave_b.append(push(src.at[c, :, cols_b], rows_b.at[me["y"], me["z"], me["c"]], y=y, c=c))
+        wave_c.append(push(src.at[c, :, cols_c], rows_c.at[me["x"], me["z"], me["c"]], z=z, c=c))
+        cols_a = pl.ds(pl.multiple_of(z * BLOCK_A, BLOCK_A), BLOCK_A)
+        wave_a.append(push(src.at[c, :, cols_a], recv_a.at[me["z"], me["c"]], z=z, c=c))
+    codes_wave = [push(codes_in.at[:, :, step("x", k)], t1.at[me["x"]], x=step("x", k)) for k in (2, 1, 3)]
+    rows_b[me["y"], me["z"], me["c"]] = src[me["c"], :, cols_b]
+    rows_c[me["x"], me["z"], me["c"]] = src[me["c"], :, cols_c]
+    recv_a[me["z"], me["c"]] = src[me["c"], :, pl.ds(pl.multiple_of(me["z"] * BLOCK_A, BLOCK_A), BLOCK_A)]
+
     def pack(pieces):
         return jnp.concatenate([p.astype(F32) for p in pieces], axis=0).astype(BF16)
 
-    wave_b = spread(rows_b.at[me["y"], me["z"]], rows_b.at[me["y"], me["z"]], "y")
-    wave_c = spread(rows_c.at[me["x"], me["z"]], rows_c.at[me["x"], me["z"]], "z")
-    wave_a = [push(send_a.at[step("z", k)], recv_a.at[me["z"]], z=step("z", k)) for k in (2, 1, 3)]
-    recv_a[me["z"]] = send_a[me["z"]]
     own_codes.wait()
 
     for copy in wave_b:
@@ -115,12 +115,12 @@
     wave_b = spread(rows_b.at[:, me["z"]], rows_b.at[:, me["z"]], "z")
     for copy in wave_c:
         copy.wait_recv()
-    h_c[me["c"], me["x"], me["y"]] = pack([rows_c[me["x"], z] for z in range(4)])
+    h_c[me["c"], me["x"], me["y"]] = pack([rows_c[me["x"], z, c] for z in range(4) for c in range(2)])
     view = h_c.at[me["c"], me["x"], me["y"]]
     wave_c = spread(view, view, "x")
     for copy in wave_a:
         copy.wait_recv()
-    h_a[me["c"], me["z"], me["x"], me["y"]] = pack([recv_a[z] for z in range(4)])
+    h_a[me["c"], me["z"], me["x"], me["y"]] = pack([recv_a[z, c] for z in range(4) for c in range(2)])
     view = h_a.at[me["c"], me["z"], me["x"], me["y"]]
     plane = [(i, k) for i in range(4) for k in range(4) if (i, k) != (0, 0)]
     wave_a = [push(view, view, x=step("x", i), y=step("y", k)) for i, k in plane]
@@ -154,9 +154,12 @@
 
     def start_ring(i):
         here = me[ring_axis[i]]
-        up0, down1 = ring(i, here, half0, 1), ring(i, here, half1, 3)
-        right[i] = [up0, ring(i, here, half1, 1)]
-        left[i] = [ring(i, here, half0, 3), down1]
+        right[i], left[i] = [], []
+        for n in range(2):
+            right[i].append(ring(i, here, n, 1))
+            left[i].append(ring(i, here, 3 - n, 3))
+        right[i].append(ring(i, here, half1, 1))
+        left[i].append(ring(i, here, half0, 3))
 
     for copy in wave_c:
         copy.wait_recv()
@@ -164,7 +167,7 @@
     for copy in wave_b:
         copy.wait_recv()
     for y in range(4):
-        h_b[me["c"], me["x"], y] = pack([rows_b[y, z] for z in range(4)])
+        h_b[me["c"], me["x"], y] = pack([rows_b[y, z, c] for z in range(4) for c in range(2)])
     start_ring(1)
     for copy in wave_a:
         copy.wait_recv()
@@ -175,54 +178,51 @@
         copy.wait_recv()
     codes_wave = [push(t2.at[:, :, :, step("z", k)], t3.at[me["z"]], z=step("z", k)) for k in (2, 1, 3)]
     t3[me["z"]] = t2[:, :, :, me["z"]]
-    forward = [None] * 3
+    forward = [[], [], []]
+    for n in range(2):
+        for i in (2, 1, 0):
+            right[i][n].wait_recv()
+            forward[i].append(ring(i, step(ring_axis[i], 3), n, 1))
+            left[i][n].wait_recv()
+            forward[i].append(ring(i, step(ring_axis[i], 1), 3 - n, 3))
     for i in (2, 1, 0):
-        right[i][0].wait_recv()
-        up = ring(i, step(ring_axis[i], 3), half0, 1)
-        left[i][1].wait_recv()
-        forward[i] = (up, ring(i, step(ring_axis[i], 1), half1, 3))
-    for i in (2, 1, 0):
-        right[i][1].wait_recv()
+        right[i][2].wait_recv()
         cross(i, step(ring_axis[i], 3))
-        left[i][0].wait_recv()
+        left[i][2].wait_recv()
         cross(i, step(ring_axis[i], 1))
     for copy in codes_wave:
         copy.wait_recv()
     codes_core = push(t3.at[:, :, :, other_core], t4.at[me["c"]], c=other_core)
     t4[me["c"]] = t3[:, :, :, me["c"]]
+    codes_core.wait_recv()
+    for x in range(4):
+        for y in range(4):
+            teacher[pl.ds((x * 4 + y) * 16, 16), :] = jnp.concatenate(
+                [t4[c, z, y, x].astype(F32) for z in range(4) for c in range(2)], axis=0
+            )
     for i in (2, 1, 0):
-        forward[i][0].wait_recv()
-        cross(i, step(ring_axis[i], 2), half0)
-        forward[i][1].wait_recv()
-        cross(i, step(ring_axis[i], 2), half1)
+        for copy in forward[i]:
+            copy.wait_recv()
+        cross(i, step(ring_axis[i], 2))
 
     w_copy.wait()
     logits[...] = jnp.zeros_like(logits)
 
     def add_logits(c):
-        for ref, first, width in ((h_b, WIDE, WIDE), (h_c, 2 * WIDE, HIDDEN_C)):
+        for ref, first, width in ((h_b, PART_A, WIDE), (h_c, PART_A + WIDE, HIDDEN_C)):
             rows = ref[c, :, :, :, pl.ds(0, width)].reshape(256, width)
             logits[...] += jnp.dot(rows, w_all[c, pl.ds(first, width), :], preferred_element_type=F32)
         rows = jnp.concatenate([h_a[c, z].reshape(256, BLOCK_A) for z in range(4)], axis=1)
-        logits[...] += jnp.dot(rows, w_all[c, pl.ds(0, WIDE), :], preferred_element_type=F32)
+        logits[...] += jnp.dot(rows, w_all[c, pl.ds(0, PART_A), :], preferred_element_type=F32)
 
     add_logits(me["c"])
-    block_row = lax.broadcasted_iota(jnp.int32, (512, 512), 0)
-    column = lax.broadcasted_iota(jnp.int32, (512, 512), 1)
-    pick = (block_row == dp * 128 + vo * 4 + column // 128).astype(F32).astype(BF16)
-    scale = jnp.dot(
-        h_c[me["c"], :, :, :, pl.ds(HIDDEN_C, 512)].reshape(256, 512), pick, preferred_element_type=F32
-    )
-    codes_core.wait_recv()
-    for x in range(4):
-        for y in range(4):
-            row = (x * 4 + y) * 16
-            code = jnp.concatenate(
-                [t4[c, z, y, x].astype(F32) for z in range(4) for c in range(2)], axis=0
-            )
-            teacher[pl.ds(row, 16), :] = code * scale[row : row + 16]
     for copy in crossing:
         copy.wait_recv()
+    block_row = lax.broadcasted_iota(jnp.int32, (256, 512), 0)
+    column = lax.broadcasted_iota(jnp.int32, (256, 512), 1)
+    pick = (block_row == (dp % 2) * 128 + vo * 4 + column // 128).astype(F32).astype(BF16)
+    scales = h_c[dp // 2, :, :, :, pl.ds(HIDDEN_C, 256)].reshape(256, 256)
+    teacher[...] *= jnp.dot(scales, pick, preferred_element_type=F32)
     add_logits(other_core)
 
     lg, tc = logits[...], teacher[...]
@@ -255,9 +255,9 @@
 
     def transpose_half(c):
         for z in range(4):
-            ht_out[pl.ds(c * HALF + z * BLOCK_A, BLOCK_A), :] = h_a[c, z].reshape(256, BLOCK_A).T
-        for ref, first, width in ((h_b, WIDE, WIDE), (h_c, 2 * WIDE, HIDDEN_C)):
-            ht_out[pl.ds(c * HALF + first, width), :] = ref[c, :, :, :, pl.ds(0, width)].reshape(256, width).T
+            ht[pl.ds(c * HALF + z * BLOCK_A, BLOCK_A), :] = h_a[c, z].reshape(256, BLOCK_A).T
+        for ref, first, width in ((h_b, PART_A, WIDE), (h_c, PART_A + WIDE, HIDDEN_C)):
+            ht[pl.ds(c * HALF + first, width), :] = ref[c, :, :, :, pl.ds(0, width)].reshape(256, width).T
 
     st_a[0] = mine
     copies = [
@@ -285,22 +285,22 @@
         - jnp.exp(teacher[...] - columns[:, 1:2])
         - CE_WEIGHT * hit.astype(F32)
     )
-    grad_out[...] = grad.astype(BF16)
+    grad_v[...] = grad.astype(BF16)
 
     own, to, came = (own_a, own_b, own_c), (to_a, to_b, to_c), (from_a, from_b, from_c)
     summed = (sum_a, sum_b, sum_c)
     fl, fr, rl, rr = (fl_a, fl_b, fl_c), (fr_a, fr_b, fr_c), (rl_a, rl_b, rl_c), (rr_a, rr_b, rr_c)
-    widths = (BLOCK_A, WIDE // 2, HIDDEN_C // 2)
-    first_of = (0, WIDE, 2 * WIDE)
+    widths = (SUM_BLOCK, SUM_WIDE // 2, SUM_WIDE // 2)
+    first_of = (0, SUM_A, SUM_A + SUM_WIDE)
     crossing, ring_waits = {}, {}
 
     def partial_of(c, i, n):
         if i == 0:
-            first = pl.multiple_of(step("z", Z_ORDER[n]) * BLOCK_A, 128)
+            first = pl.multiple_of(step("z", Z_ORDER[n]) * SUM_BLOCK, 128)
         else:
             first = first_of[i] + n * widths[i]
         return lax.dot_general(
-            grad_out[...], w_all[c, pl.ds(first, widths[i]), :], (((1,), (1,)), ((), ())),
+            grad_v[...], w_all[c, pl.ds(first, widths[i]), :], (((1,), (1,)), ((), ())),
             preferred_element_type=F32,
         ).reshape(4, 4, 16, widths[i])
 
@@ -361,6 +361,11 @@
         ring_opposite(i, n)
         ring_up(i, n)
         ring_down(i, n)
+
+    def head_chunks(first, last):
+        for n in range(first, last):
+            chunk = pl.ds(n * CHUNK, CHUNK)
+            head_out[chunk, :] = jnp.dot(ht[chunk, :], grad_v[...], preferred_element_type=F32).astype(BF16)
 
     send_unit(0, 0)
     send_unit(1, 0)
@@ -372,26 +377,28 @@
     own_unit(1, 0)
     add_unit(1, 0)
     start_unit(1, 0)
-    send_unit(0, 1)
+    send_unit(1, 1)
     own_unit(2, 0)
     add_unit(2, 0)
     start_unit(2, 0)
-    send_unit(1, 1)
-    own_unit(0, 1)
-    add_unit(0, 1)
-    ring_down(0, 0)
     send_unit(2, 1)
     own_unit(1, 1)
     add_unit(1, 1)
     start_unit(1, 1)
-    ring_forward(0, 0)
+    send_unit(0, 1)
     own_unit(2, 1)
     add_unit(2, 1)
     start_unit(2, 1)
+    own_unit(0, 1)
+    add_unit(0, 1)
+    ring_down(0, 0)
+    ring_forward(0, 0)
+    head_chunks(0, 1)
     ring_forward(1, 0)
     ring_forward(2, 0)
     ring_forward(1, 1)
     ring_forward(2, 1)
+    head_chunks(1, 3)
 
     def ring_done(i):
         for n in range(1 if i == 0 else 2):
@@ -420,6 +427,7 @@
         acc_c[:, :, cols] = own_c[n, :, me["y"]] + rl_c[n].astype(F32) + rr_c[n].astype(F32)
     out_c[...] = acc_c[...].astype(BF16)
     wave_c = [push(out_c.at[step("x", k)], in_c.at[k - 1], x=step("x", k)) for k in (2, 1, 3)]
+    head_chunks(3, 6)
     loss_out[...] = jnp.broadcast_to(
         jnp.sum(jnp.where(reorder, columns[:, 2:3], 0.0), axis=0, keepdims=True), (8, 256)
     )
@@ -429,56 +437,63 @@
     total = keep_b[me["z"]]
     for n in range(3):
         total = total + in_b[n].astype(F32)
-    rest_b[...] = total
-    wave_b = [push(rest_b.at[step("y", k)], last_b.at[k - 1], y=step("y", k)) for k in (2, 1, 3)]
+    for c in range(2):
+        rest_b[:, c] = total[:, c * 2 : c * 2 + 2]
+
+    def last_step(rest, last, axis):
+        copies = [
+            push(rest.at[step(axis, k), step("c", e)], last.at[e * 4 + k], **{axis: step(axis, k)}, c=step("c", e))
+            for k, e in group
+        ]
+        last[0] = rest[me[axis], me["c"]]
+        return copies
+
+    wave_b = last_step(rest_b, last_b, "y")
     for copy in wave_c:
         copy.wait_recv()
     total = acc_c[me["x"]]
     for n in range(3):
         total = total + in_c[n].astype(F32)
     for z in range(4):
-        rest_c[z] = total[z * 4 : z * 4 + 4]
-    wave_c = [push(rest_c.at[step("z", k)], last_c.at[k - 1], z=step("z", k)) for k in (2, 1, 3)]
+        for c in range(2):
+            rest_c[z, c] = total[z * 4 + c * 2 : z * 4 + c * 2 + 2]
+    wave_c = last_step(rest_c, last_c, "z")
     for copy in wave_a:
         copy.wait_recv()
     total = acc_a[me["x"], me["y"]]
     for n in range(15):
         total = total + in_a[n].astype(F32)
     for z in range(4):
-        rest_a[z] = total[z * 4 : z * 4 + 4]
-    wave_a = [push(rest_a.at[step("z", k)], last_a.at[me["z"]], z=step("z", k)) for k in (2, 1, 3)]
-    last_a[me["z"]] = rest_a[me["z"]]
-
-    def finish(total, first, width):
         for c in range(2):
-            fin_s[c, :, pl.ds(first, width)] = total[c * 2 : c * 2 + 2]
-
-    for copy in wave_b:
-        copy.wait_recv()
-    finish(rest_b[me["y"]] + last_b[0] + last_b[1] + last_b[2], WIDE, WIDE)
-    for copy in wave_c:
-        copy.wait_recv()
-    finish(rest_c[me["z"]] + last_c[0] + last_c[1] + last_c[2], 2 * WIDE, HIDDEN_C)
+            rest_a[z, c] = total[z * 4 + c * 2 : z * 4 + c * 2 + 2]
+    wave_a = []
+    for k, e in group:
+        z, c = step("z", k), step("c", e)
+        wave_a.append(push(rest_a.at[z, c], last_a.at[me["z"], me["c"]], z=z, c=c))
+    last_a[me["z"], me["c"]] = rest_a[me["z"], me["c"]]
+    head_chunks(6, 8)
+
+    for wave, last, first in ((wave_b, last_b, SUM_A), (wave_c, last_c, SUM_A + SUM_WIDE)):
+        for copy in wave:
+            copy.wait_recv()
+        for e in range(2):
+            total = last[e * 4] + last[e * 4 + 1] + last[e * 4 + 2] + last[e * 4 + 3]
+            hg_out[step("c", e), :, pl.ds(first, SUM_WIDE)] = total
     for copy in wave_a:
         copy.wait_recv()
     for z in range(4):
-        finish(last_a[z], z * BLOCK_A, BLOCK_A)
-    swap = push(fin_s.at[other_core], fin_r, c=other_core)
-    hg_out[me["c"]] = fin_s[me["c"]]
-    for copy in unsent[:-1]:
+        for c in range(2):
+            hg_out[c, :, pl.ds(z * SUM_BLOCK, SUM_BLOCK)] = last_a[z, c]
+    for copy in unsent:
         copy.wait_send()
-    swap.wait_recv()
-    hg_out[other_core] = fin_r[...]
-    swap.wait_send()
-
-
-def head_kernel(ht_ref, grad_ref, hg_ref, loss_ref, out_ref, hg_out, loss_out, out_v, sems):
+
+
+def store_kernel(head_ref, hg_ref, loss_ref, head_out, hg_out, loss_out, sems):
     copies = []
-    for g in range(8):
-        out_v[g] = jnp.dot(ht_ref[pl.ds(g * CHUNK, CHUNK), :], grad_ref[...], preferred_element_type=F32).astype(BF16)
-        copy = pltpu.make_async_copy(out_v.at[g], out_ref.at[pl.ds(g * CHUNK, CHUNK)], sems.at[g])
-        copy.start()
-        copies.append(copy)
+    for n in range(8):
+        chunk = pl.ds(n * CHUNK, CHUNK)
+        copies.append(pltpu.make_async_copy(head_ref.at[chunk], head_out.at[chunk], sems.at[n]))
+        copies[n].start()
     for c in range(2):
         hg_out[:, pl.ds(c * HALF, HALF)] = hg_ref[c]
     loss_out[...] = loss_ref[0]
@@ -491,18 +506,19 @@
     weight = head_weight.reshape(2, HALF, 512)
 
     vmem = pltpu.VMEM
-    half_b, half_c = WIDE // 2, HIDDEN_C // 2
-    unit_a, unit_b, unit_c = (4, 4, 4, 16, BLOCK_A), (2, 4, 4, 16, half_b), (2, 4, 4, 16, half_c)
-    forwarded = ((2, 4, 16, BLOCK_A), (2, 2, 16, half_b), (2, 2, 16, half_c))
-    arrived = ((4, 4, 16, BLOCK_A), (2, 4, 16, half_b), (2, 4, 16, half_c))
+    unit_a, unit_b = (4, 4, 4, 16, SUM_BLOCK), (2, 4, 4, 16, SUM_WIDE // 2)
+    forwarded_a, forwarded_b = (2, 4, 16, SUM_BLOCK), (2, 2, 16, SUM_WIDE // 2)
+    arrived_a, arrived_b = (4, 4, 16, SUM_BLOCK), (2, 4, 16, SUM_WIDE // 2)
+    units = (unit_a, unit_b, unit_b)
+    forwarded, arrived = (forwarded_a, forwarded_b, forwarded_b), (arrived_a, arrived_b, arrived_b)
     scratch = [
         vmem((2, HALF, 512), BF16),
-        vmem((2, 2, HALF + 512), BF16),
-        vmem((2, 2, HALF + 512), BF16),
-        vmem((4, 4, BLOCK_A), BF16),
-        vmem((4, 4, BLOCK_A), BF16),
-        vmem((4, 4, 4, WIDE), BF16),
-        vmem((4, 4, 4, WIDE), BF16),
+        vmem((256, 512), BF16),
+        vmem((8192, 256), BF16),
+        vmem((2, 2, HALF + 256), BF16),
+        vmem((4, 2, 2, BLOCK_A), BF16),
+        vmem((4, 4, 2, 2, WIDE), BF16),
+        vmem((4, 4, 2, 2, WIDE), BF16),
         vmem((2, 4, 4, 4, 16, BLOCK_A), BF16),
         vmem((2, 4, 4, 16, WIDE), BF16),
         vmem((2, 4, 4, 16, WIDE), BF16),
@@ -515,60 +531,57 @@
         vmem((8, 8, 256), F32),
         vmem((16, 8, 256), F32),
     ]
-    scratch += [vmem(shape, F32) for shape in (unit_a, unit_b, unit_c)]
-    scratch += [vmem(shape, BF16) for shape in (unit_a, unit_b, unit_c) * 3]
+    scratch += [vmem(shape, F32) for shape in units]
+    scratch += [vmem(shape, BF16) for shape in units * 3]
     scratch += [vmem(shape, BF16) for shape in forwarded * 2 + arrived * 2]
     scratch += [
-        vmem((4, 4, 16, BLOCK_A), F32),
-        vmem((4, 16, WIDE), F32),
-        vmem((4, 16, HIDDEN_C), F32),
-        vmem((4, 4, 16, BLOCK_A), BF16),
-        vmem((4, 4, 4, WIDE), BF16),
-        vmem((4, 16, HIDDEN_C), BF16),
-        vmem((15, 16, BLOCK_A), BF16),
-        vmem((3, 4, 4, WIDE), BF16),
-        vmem((3, 16, HIDDEN_C), BF16),
-        vmem((4, 4, 4, WIDE), F32),
-        vmem((4, 4, BLOCK_A), F32),
-        vmem((4, 4, WIDE), F32),
-        vmem((4, 4, HIDDEN_C), F32),
-        vmem((4, 4, BLOCK_A), F32),
-        vmem((3, 4, WIDE), F32),
-        vmem((3, 4, HIDDEN_C), F32),
-        vmem((2, 2, HALF), F32),
-        vmem((2, HALF), F32),
-        pltpu.SemaphoreType.DMA((208,)),
-        pltpu.SemaphoreType.DMA((208,)),
+        vmem((4, 4, 16, SUM_BLOCK), F32),
+        vmem((4, 16, SUM_WIDE), F32),
+        vmem((4, 16, SUM_WIDE), F32),
+        vmem((4, 4, 16, SUM_BLOCK), BF16),
+        vmem((4, 4, 4, SUM_WIDE), BF16),
+        vmem((4, 16, SUM_WIDE), BF16),
+        vmem((15, 16, SUM_BLOCK), BF16),
+        vmem((3, 4, 4, SUM_WIDE), BF16),
+        vmem((3, 16, SUM_WIDE), BF16),
+        vmem((4, 4, 4, SUM_WIDE), F32),
+        vmem((4, 2, 2, SUM_BLOCK), F32),
+        vmem((4, 2, 2, SUM_WIDE), F32),
+        vmem((4, 2, 2, SUM_WIDE), F32),
+        vmem((4, 2, 2, SUM_BLOCK), F32),
+        vmem((8, 2, SUM_WIDE), F32),
+        vmem((8, 2, SUM_WIDE), F32),
+        pltpu.SemaphoreType.DMA((248,)),
+        pltpu.SemaphoreType.DMA((248,)),
         pltpu.SemaphoreType.DMA((8,)),
     ]
-    hidden_grad, loss, grad, hidden_t = pl.pallas_call(
+    hidden_grad, loss, head_grad = pl.pallas_call(
         kernel,
         out_shape=(
             pltpu.VMEM((2, 2, HALF), F32),
             pltpu.VMEM((8, 256), F32),
-            pltpu.VMEM((256, 512), BF16),
-            pltpu.VMEM((8192, 256), BF16),
+            pltpu.VMEM((8192, 512), BF16),
         ),
         in_specs=[pl.BlockSpec(memory_space=pltpu.HBM)] * 4 + [pl.BlockSpec(memory_space=pltpu.VMEM)],
-        out_specs=[pl.BlockSpec(memory_space=pltpu.VMEM)] * 4,
+        out_specs=[pl.BlockSpec(memory_space=pltpu.VMEM)] * 3,
         scratch_shapes=scratch,
         compiler_params=pltpu.CompilerParams(
-            collective_id=0, has_side_effects=True, vmem_limit_bytes=61500000
+            collective_id=0, has_side_effects=True, vmem_limit_bytes=57500000
         ),
     )(hidden_states, weight, codes, teacher_scales, targets.reshape(1, 256))
 
     head_grad, hidden_grad, token_loss = pl.pallas_call(
-        head_kernel,
+        store_kernel,
         out_shape=(
             jax.ShapeDtypeStruct((8192, 512), BF16),
             jax.ShapeDtypeStruct((2, 8192), F32),
             jax.ShapeDtypeStruct((256,), F32),
         ),
-        in_specs=[pl.BlockSpec(memory_space=pltpu.VMEM)] * 4,
+        in_specs=[pl.BlockSpec(memory_space=pltpu.VMEM)] * 3,
         out_specs=[pl.BlockSpec(memory_space=pltpu.HBM)] + [pl.BlockSpec(memory_space=pltpu.VMEM)] * 2,
-        scratch_shapes=[pltpu.VMEM((8, CHUNK, 512), BF16), pltpu.SemaphoreType.DMA((8,))],
+        scratch_shapes=[pltpu.SemaphoreType.DMA((8,))],
         compiler_params=pltpu.CompilerParams(vmem_limit_bytes=40 * 1024 * 1024),
-    )(hidden_t, grad, hidden_grad, loss)
+    )(head_grad, hidden_grad, loss)
     return hidden_grad, head_grad, token_loss
 
 

time: 77.1 us -> 75.1 us (0.974)
  Pallas kernels: 76.3 us -> 74.2 us
    pallas_call x1, Pallas kernels: 71.9 us -> 70.2 us  [per_device(): pl.pallas_call(kernel, out_shape=(pltpu.VMEM((2, 2, HALF), F32), pltpu.VM...]
where the time goes in v5:
time: 75.1 us; the launch traced here: 74.9 us
  Pallas kernels  74.2 us (99%)
    pallas_call x1, Pallas kernels, per_device(): pl.pallas_call(kernel, out_shape=(pltpu.VMEM((2, 2, HALF), F32), pltpu.VM...  70.2 us
    pallas_call x1, Pallas kernels, per_device(): pl.pallas_call(store_kernel, out_shape=(jax.ShapeDtypeStruct((8192, 512),...  4 us

profile of v5, /device:TPU:1, one launch (start us, length us, event | category | flops | bytes accessed | tf_op | source)
XLA Modules:
  0.0 74.9 jit_solution(4010322990217642281)
XLA Ops:
  0.6 70.2 %shard_map.76 = (f32[2,2,4096]{2,1,0:T(2,128)S(1)}, f32[8,256]{1,0:T(8,128)S(1)}, bf16[8192,512]{1,0:T(8,128)(2,1)S(1)}) custom-call(bf16[2,8192]{1,0:T(2,128)(2,1)} %h_in.1, bf16[2,4096,512]{2,1,0:T(8,128)(2,1)} %bitcast.7, bf16[2,2,4,4,2,2,512]{6,5,4,3,2,1,0:T(2,128)(2,1)} %bitcast.8, bf16[2,512]{1,0:T(2,128)(2,1)} %scales_in.1, s32[1,256]{1,0:T(1,128)} %bitcast.9), custom_call_target="tpu_custom_call" | custom-call | tf_op jit(solution)/shard_map/pallas_call | solution.py:558
  70.9 4.0 %shard_map.77 = (bf16[8192,512]{1,0:T(8,128)(2,1)}, f32[2,8192]{1,0:T(2,128)}, f32[256]{0:T(256)}) custom-call(bf16[8192,512]{1,0:T(8,128)(2,1)S(1)} %get-tuple-element.9.head_ref, f32[2,2,4096]{2,1,0:T(2,128)S(1)} %get-tuple-element.10.hg_ref, f32[8,256]{1,0:T(8,128)S(1)} %get-tuple-element.11.loss_ref), custom_call_target="tpu_custom_call" | custom-call | tf_op jit(solution)/shard_map/pallas_call | solution.py:573

commit v6 on v5

--- a/solution.py
+++ b/solution.py
@@ -26,7 +26,7 @@
     w_all, grad_v, ht, src, recv_a, rows_b, rows_c, h_a, h_b, h_c,
     t1, t2, t3, t4, logits, teacher, st_a, st_b,
     own_a, own_b, own_c, to_a, to_b, to_c, from_a, from_b, from_c, sum_a, sum_b, sum_c,
-    fl_a, fl_b, fl_c, fr_a, fr_b, fr_c, rl_a, rl_b, rl_c, rr_a, rr_b, rr_c,
+    fl_a, fl_b, fl_c, fr_a, fr_b, fr_c, rl_a, rl_b, rl_c, rr_a, rr_b, rr_c, ro_b, ro_c,
     acc_a, acc_b, acc_c, out_a, out_b, out_c, in_a, in_b, in_c, keep_b,
     rest_a, rest_b, rest_c, last_a, last_b, last_c,
     send_sems, recv_sems, local_sems,
@@ -164,6 +164,10 @@
     for copy in wave_c:
         copy.wait_recv()
     start_ring(2)
+    for copy in codes_wave:
+        copy.wait_recv()
+    codes_wave = [push(t2.at[:, :, :, step("z", k)], t3.at[me["z"]], z=step("z", k)) for k in (2, 1, 3)]
+    t3[me["z"]] = t2[:, :, :, me["z"]]
     for copy in wave_b:
         copy.wait_recv()
     for y in range(4):
@@ -174,10 +178,6 @@
     start_ring(0)
     for i in (2, 1, 0):
         cross(i, me[ring_axis[i]])
-    for copy in codes_wave:
-        copy.wait_recv()
-    codes_wave = [push(t2.at[:, :, :, step("z", k)], t3.at[me["z"]], z=step("z", k)) for k in (2, 1, 3)]
-    t3[me["z"]] = t2[:, :, :, me["z"]]
     forward = [[], [], []]
     for n in range(2):
         for i in (2, 1, 0):
@@ -362,6 +362,13 @@
         ring_up(i, n)
         ring_down(i, n)
 
+    def start_last(i):
+        axis = ring_axis[i]
+        ring_waits[i, 1] = [None, None] + [
+            push(summed[i].at[block_of(i, k, 1, full)], target, **{axis: step(axis, k)})
+            for k, target in ((2, (None, ro_b, ro_c)[i]), (1, rl[i].at[1]), (3, rr[i].at[1]))
+        ]
+
     def head_chunks(first, last):
         for n in range(first, last):
             chunk = pl.ds(n * CHUNK, CHUNK)
@@ -369,36 +376,33 @@
 
     send_unit(0, 0)
     send_unit(1, 0)
+    send_unit(2, 0)
     own_unit(0, 0)
+    send_unit(1, 1)
+    own_unit(1, 0)
+    send_unit(2, 1)
     add_unit(0, 0)
     ring_opposite(0, 0)
     ring_up(0, 0)
-    send_unit(2, 0)
-    own_unit(1, 0)
+    send_unit(0, 1)
     add_unit(1, 0)
     start_unit(1, 0)
-    send_unit(1, 1)
     own_unit(2, 0)
     add_unit(2, 0)
     start_unit(2, 0)
-    send_unit(2, 1)
     own_unit(1, 1)
     add_unit(1, 1)
-    start_unit(1, 1)
-    send_unit(0, 1)
+    start_last(1)
     own_unit(2, 1)
     add_unit(2, 1)
-    start_unit(2, 1)
+    start_last(2)
     own_unit(0, 1)
     add_unit(0, 1)
     ring_down(0, 0)
     ring_forward(0, 0)
-    head_chunks(0, 1)
     ring_forward(1, 0)
     ring_forward(2, 0)
-    ring_forward(1, 1)
-    ring_forward(2, 1)
-    head_chunks(1, 3)
+    head_chunks(0, 3)
 
     def ring_done(i):
         for n in range(1 if i == 0 else 2):
@@ -415,7 +419,8 @@
     ring_done(1)
     for n in range(2):
         cols = pl.ds(n * widths[1], widths[1])
-        acc_b[:, :, cols] = own_b[n, me["x"]] + rl_b[n].astype(F32) + rr_b[n].astype(F32)
+        total = own_b[n, me["x"]] + rl_b[n].astype(F32) + rr_b[n].astype(F32)
+        acc_b[:, :, cols] = total + ro_b[...].astype(F32) if n else total
     for z in range(4):
         piece = acc_b[:, pl.ds(z * 4, 4), :]
         keep_b[z] = piece
@@ -424,7 +429,8 @@
     ring_done(2)
     for n in range(2):
         cols = pl.ds(n * widths[2], widths[2])
-        acc_c[:, :, cols] = own_c[n, :, me["y"]] + rl_c[n].astype(F32) + rr_c[n].astype(F32)
+        total = own_c[n, :, me["y"]] + rl_c[n].astype(F32) + rr_c[n].astype(F32)
+        acc_c[:, :, cols] = total + ro_c[...].astype(F32) if n else total
     out_c[...] = acc_c[...].astype(BF16)
     wave_c = [push(out_c.at[step("x", k)], in_c.at[k - 1], x=step("x", k)) for k in (2, 1, 3)]
     head_chunks(3, 6)
@@ -533,7 +539,7 @@
     ]
     scratch += [vmem(shape, F32) for shape in units]
     scratch += [vmem(shape, BF16) for shape in units * 3]
-    scratch += [vmem(shape, BF16) for shape in forwarded * 2 + arrived * 2]
+    scratch += [vmem(shape, BF16) for shape in forwarded * 2 + arrived * 2 + (arrived_b[1:],) * 2]
     scratch += [
         vmem((4, 4, 16, SUM_BLOCK), F32),
         vmem((4, 16, SUM_WIDE), F32),

time: 75.1 us -> 73.8 us (0.983)
  Pallas kernels: 74.2 us -> 73 us
    pallas_call x1, Pallas kernels: 70.2 us -> 69 us  [per_device(): pl.pallas_call(kernel, out_shape=(pltpu.VMEM((2, 2, HALF), F32), pltpu.VM...]
where the time goes in v6:
time: 73.8 us; the launch traced here: 73.6 us
  Pallas kernels  73 us (99%)
    pallas_call x1, Pallas kernels, per_device(): pl.pallas_call(kernel, out_shape=(pltpu.VMEM((2, 2, HALF), F32), pltpu.VM...  69 us
    pallas_call x1, Pallas kernels, per_device(): pl.pallas_call(store_kernel, out_shape=(jax.ShapeDtypeStruct((8192, 512),...  4 us

profile of v6, /device:TPU:1, one launch (start us, length us, event | category | flops | bytes accessed | tf_op | source)
XLA Modules:
  0.0 73.6 jit_solution(4586211360539454861)
XLA Ops:
  0.6 69.0 %shard_map.76 = (f32[2,2,4096]{2,1,0:T(2,128)S(1)}, f32[8,256]{1,0:T(8,128)S(1)}, bf16[8192,512]{1,0:T(8,128)(2,1)S(1)}) custom-call(bf16[2,8192]{1,0:T(2,128)(2,1)} %h_in.1, bf16[2,4096,512]{2,1,0:T(8,128)(2,1)} %bitcast.7, bf16[2,2,4,4,2,2,512]{6,5,4,3,2,1,0:T(2,128)(2,1)} %bitcast.8, bf16[2,512]{1,0:T(2,128)(2,1)} %scales_in.1, s32[1,256]{1,0:T(1,128)} %bitcast.9), custom_call_target="tpu_custom_call" | custom-call | tf_op jit(solution)/shard_map/pallas_call | solution.py:564
  69.6 4.0 %shard_map.77 = (bf16[8192,512]{1,0:T(8,128)(2,1)}, f32[2,8192]{1,0:T(2,128)}, f32[256]{0:T(256)}) custom-call(bf16[8192,512]{1,0:T(8,128)(2,1)S(1)} %get-tuple-element.9.head_ref, f32[2,2,4096]{2,1,0:T(2,128)S(1)} %get-tuple-element.10.hg_ref, f32[8,256]{1,0:T(8,128)S(1)} %get-tuple-element.11.loss_ref), custom_call_target="tpu_custom_call" | custom-call | tf_op jit(solution)/shard_map/pallas_call | solution.py:579

commit v7 on v6

--- a/solution.py
+++ b/solution.py
@@ -15,7 +15,7 @@
 
 CHUNK = 1024
 HALF = 4096
-BLOCK_A, PART_A, WIDE, HIDDEN_C = 256, 1024, 1664, 1408
+BLOCK_A, PART_A, WIDE, HIDDEN_C = 128, 512, 1920, 1664
 SUM_BLOCK, SUM_A, SUM_WIDE = 384, 1536, 1280
 Z_ORDER = (2, 1, 3, 0)
 
@@ -54,6 +54,11 @@
         copy.start()
         unsent.append(copy)
         return copy
+
+    def drain(keep=0):
+        for copy in unsent[: len(unsent) - keep]:
+            copy.wait_send()
+        del unsent[: len(unsent) - keep]
 
     def local(src, dst):
         n = count["local"]
@@ -194,28 +199,28 @@
         copy.wait_recv()
     codes_core = push(t3.at[:, :, :, other_core], t4.at[me["c"]], c=other_core)
     t4[me["c"]] = t3[:, :, :, me["c"]]
+    for i in (2, 1, 0):
+        for copy in forward[i]:
+            copy.wait_recv()
+        cross(i, step(ring_axis[i], 2))
+
+    w_copy.wait()
+    logits[...] = jnp.zeros_like(logits)
+
+    def add_logits(c):
+        for ref, first, width in ((h_b, PART_A, WIDE), (h_c, PART_A + WIDE, HIDDEN_C)):
+            rows = ref[c, :, :, :, pl.ds(0, width)].reshape(256, width)
+            logits[...] += jnp.dot(rows, w_all[c, pl.ds(first, width), :], preferred_element_type=F32)
+        rows = jnp.concatenate([h_a[c, z].reshape(256, BLOCK_A) for z in range(4)], axis=1)
+        logits[...] += jnp.dot(rows, w_all[c, pl.ds(0, PART_A), :], preferred_element_type=F32)
+
+    add_logits(me["c"])
     codes_core.wait_recv()
     for x in range(4):
         for y in range(4):
             teacher[pl.ds((x * 4 + y) * 16, 16), :] = jnp.concatenate(
                 [t4[c, z, y, x].astype(F32) for z in range(4) for c in range(2)], axis=0
             )
-    for i in (2, 1, 0):
-        for copy in forward[i]:
-            copy.wait_recv()
-        cross(i, step(ring_axis[i], 2))
-
-    w_copy.wait()
-    logits[...] = jnp.zeros_like(logits)
-
-    def add_logits(c):
-        for ref, first, width in ((h_b, PART_A, WIDE), (h_c, PART_A + WIDE, HIDDEN_C)):
-            rows = ref[c, :, :, :, pl.ds(0, width)].reshape(256, width)
-            logits[...] += jnp.dot(rows, w_all[c, pl.ds(first, width), :], preferred_element_type=F32)
-        rows = jnp.concatenate([h_a[c, z].reshape(256, BLOCK_A) for z in range(4)], axis=1)
-        logits[...] += jnp.dot(rows, w_all[c, pl.ds(0, PART_A), :], preferred_element_type=F32)
-
-    add_logits(me["c"])
     for copy in crossing:
         copy.wait_recv()
     block_row = lax.broadcasted_iota(jnp.int32, (256, 512), 0)
@@ -263,6 +268,7 @@
     copies = [
         push(st_a.at[0], st_a.at[1 + n], z=step("z", k), c=step("c", e)) for n, (k, e) in enumerate(group)
     ]
+    drain(len(copies))
     transpose_half(0)
     for copy in copies:
         copy.wait_recv()
@@ -271,6 +277,7 @@
     copies = [
         push(st_b.at[0], st_b.at[1 + n], x=step("x", i), y=step("y", k)) for n, (i, k) in enumerate(plane)
     ]
+    drain(len(copies))
     transpose_half(1)
     for copy in copies:
         copy.wait_recv()
@@ -433,6 +440,7 @@
         acc_c[:, :, cols] = total + ro_c[...].astype(F32) if n else total
     out_c[...] = acc_c[...].astype(BF16)
     wave_c = [push(out_c.at[step("x", k)], in_c.at[k - 1], x=step("x", k)) for k in (2, 1, 3)]
+    drain(len(wave_a) + len(wave_b) + len(wave_c))
     head_chunks(3, 6)
     loss_out[...] = jnp.broadcast_to(
         jnp.sum(jnp.where(reorder, columns[:, 2:3], 0.0), axis=0, keepdims=True), (8, 256)
@@ -477,6 +485,7 @@
         z, c = step("z", k), step("c", e)
         wave_a.append(push(rest_a.at[z, c], last_a.at[me["z"], me["c"]], z=z, c=c))
     last_a[me["z"], me["c"]] = rest_a[me["z"], me["c"]]
+    drain(len(wave_a) + len(wave_b) + len(wave_c))
     head_chunks(6, 8)
 
     for wave, last, first in ((wave_b, last_b, SUM_A), (wave_c, last_c, SUM_A + SUM_WIDE)):
@@ -490,8 +499,7 @@
     for z in range(4):
         for c in range(2):
             hg_out[c, :, pl.ds(z * SUM_BLOCK, SUM_BLOCK)] = last_a[z, c]
-    for copy in unsent:
-        copy.wait_send()
+    drain()
 
 
 def store_kernel(head_ref, hg_ref, loss_ref, head_out, hg_out, loss_out, sems):

time: 73.8 us -> 72.6 us (0.984)
  Pallas kernels: 73 us -> 71.8 us
    pallas_call x1, Pallas kernels: 69 us -> 67.8 us  [per_device(): pl.pallas_call(kernel, out_shape=(pltpu.VMEM((2, 2, HALF), F32), pltpu.VM...]
where the time goes in v7:
time: 72.6 us; the launch traced here: 72.4 us
  Pallas kernels  71.8 us (99%)
    pallas_call x1, Pallas kernels, per_device(): pl.pallas_call(kernel, out_shape=(pltpu.VMEM((2, 2, HALF), F32), pltpu.VM...  67.8 us
    pallas_call x1, Pallas kernels, per_device(): pl.pallas_call(store_kernel, out_shape=(jax.ShapeDtypeStruct((8192, 512),...  4 us

profile of v7, /device:TPU:1, one launch (start us, length us, event | category | flops | bytes accessed | tf_op | source)
XLA Modules:
  0.0 72.4 jit_solution(10638761627232431179)
XLA Ops:
  0.6 67.8 %shard_map.76 = (f32[2,2,4096]{2,1,0:T(2,128)S(1)}, f32[8,256]{1,0:T(8,128)S(1)}, bf16[8192,512]{1,0:T(8,128)(2,1)S(1)}) custom-call(bf16[2,8192]{1,0:T(2,128)(2,1)} %h_in.1, bf16[2,4096,512]{2,1,0:T(8,128)(2,1)} %bitcast.7, bf16[2,2,4,4,2,2,512]{6,5,4,3,2,1,0:T(2,128)(2,1)} %bitcast.8, bf16[2,512]{1,0:T(2,128)(2,1)} %scales_in.1, s32[1,256]{1,0:T(1,128)} %bitcast.9), custom_call_target="tpu_custom_call" | custom-call | tf_op jit(solution)/shard_map/pallas_call | solution.py:572
  68.4 4.0 %shard_map.77 = (bf16[8192,512]{1,0:T(8,128)(2,1)}, f32[2,8192]{1,0:T(2,128)}, f32[256]{0:T(256)}) custom-call(bf16[8192,512]{1,0:T(8,128)(2,1)S(1)} %get-tuple-element.9.head_ref, f32[2,2,4096]{2,1,0:T(2,128)S(1)} %get-tuple-element.10.hg_ref, f32[8,256]{1,0:T(8,128)S(1)} %get-tuple-element.11.loss_ref), custom_call_target="tpu_custom_call" | custom-call | tf_op jit(solution)/shard_map/pallas_call | solution.py:587
